TPU v7x, 256 devices: a whole 4x4x8 slice. The times are simulated.
256 devices in a mesh: ka: 128 (over z, x_lo, y, core), aux: 2 (over x_hi).
Axes of the slice: x: 4 (x_hi: 2, x_lo: 2; x = x_hi * 2 + x_lo), y: 4, z: 8, core: 2. Of those that a mesh axis runs over, the one named last changes fastest.
Arguments:
- coefficients: bfloat16 [128, 4096, 128], P('ka'), may hold values from -2.09375 to 2.09375
- triple: bfloat16 [64, 2, 64, 768], P('aux'), may hold values from -0.5 to 0.5
- neighbors: int32 [64, 2], P('aux'), may hold values from 0 to 63
- w_screened: bfloat16 [128, 768, 1536], P('ka', 'aux'), as said below
- partner: int32 [2, 128], replicated, may hold values from 0 to 127, each once within a row
- q_ids: int32 [2], replicated, may hold values from 0 to 127
Outputs:
- sigma: float32 [128, 64, 128], P('ka', 'aux')
Inputs may be any that keep to these rules, and one draw needn't show every extreme that they name: Each stored w_screened is Hermitian: its real block is symmetric and its imaginary block antisymmetric.
All inputs are finite; a program needn't handle non-finite values.
Results may differ from a plain program's by a relative error of at most 0.0085.
Values may be sent and summed in bfloat16 or wider, within the bound.
No kernel may reach another device: no remote copies, remote signals or barrier semaphores. Data moves between devices by JAX's collectives and lax.ppermute only.
A program may use at most 128 MiB of HBM per device.

v0:
```python
import math

import jax
import jax.numpy as jnp
from jax import lax
from jax.sharding import PartitionSpec as P

CELL_ATOMS = 64
ORBITALS_PER_ATOM = 64
AUX_ATOM = 12
OCCUPIED_BANDS = 16
TRANSFERS = 2
NAUX = 768


def from_root(block, axis, source):
    block = jnp.where(lax.axis_index(axis) == source, block, jnp.zeros_like(block))
    return lax.psum(block, axis)


def rotated_parts(values, band_count):
    return jnp.concatenate([-values[..., band_count:], values[..., :band_count]], axis=-1)


def sigma_parts(blocks, band_count):
    sigma_real = blocks[:, :band_count, :band_count] + blocks[:, band_count:, band_count:]
    sigma_imag = blocks[:, :band_count, band_count:] - blocks[:, band_count:, :band_count]
    return (sigma_real, sigma_imag)


def local(coefficients, triple, neighbors, w_screened, partner, q_ids):
    kpoints, orbitals, doubled = coefficients.shape
    band_count = doubled // 2
    local_atoms = triple.shape[0]
    local_aux = local_atoms * AUX_ATOM
    half_index = lax.axis_index("aux")
    prefactor = -1.0 / math.sqrt(TRANSFERS * NAUX * OCCUPIED_BANDS)
    screens = [
        from_root(w_screened[0], "ka", q_ids[momentum_transfer])
        for momentum_transfer in range(TRANSFERS)
    ]
    far_cols = jnp.concatenate(
        [
            coefficients[:, :, :OCCUPIED_BANDS],
            coefficients[:, :, band_count : band_count + OCCUPIED_BANDS],
        ],
        axis=2,
    )
    packed = far_cols.reshape(kpoints, orbitals * 2 * OCCUPIED_BANDS // 128, 128)
    spread = lax.all_to_all(packed, "ka", split_axis=1, concat_axis=0, tiled=True)
    permuted = jnp.take(spread, partner, axis=0)
    arrived = jnp.stack(
        [
            lax.all_to_all(
                permuted[momentum_transfer], "ka", split_axis=0, concat_axis=1, tiled=True
            )
            for momentum_transfer in range(TRANSFERS)
        ]
    )
    distant_coefficients = arrived.reshape(
        TRANSFERS, kpoints, CELL_ATOMS, ORBITALS_PER_ATOM, 2 * OCCUPIED_BANDS
    )
    own_rows = lax.dynamic_slice_in_dim(
        coefficients,
        half_index * local_atoms * ORBITALS_PER_ATOM,
        local_atoms * ORBITALS_PER_ATOM,
        1,
    )
    home_coefficients = own_rows.reshape(kpoints, local_atoms, ORBITALS_PER_ATOM, doubled)
    neighbour_coef = jnp.take(distant_coefficients, neighbors, axis=2)
    pair_half = jnp.einsum(
        "tkcjoy,cjox->tkcyx", neighbour_coef, triple, preferred_element_type=jnp.float32
    ).astype(jnp.bfloat16)
    pair_half = pair_half.reshape(
        TRANSFERS, kpoints, local_atoms, 2 * OCCUPIED_BANDS, AUX_ATOM, ORBITALS_PER_ATOM
    )
    combos = jnp.einsum(
        "kcix,tkcyai->tkcayx", home_coefficients, pair_half, preferred_element_type=jnp.float32
    )
    real_part = (
        combos[..., :OCCUPIED_BANDS, :band_count] + combos[..., OCCUPIED_BANDS:, band_count:]
    )
    imag_part = (
        combos[..., OCCUPIED_BANDS:, :band_count] - combos[..., :OCCUPIED_BANDS, band_count:]
    )
    products = jnp.concatenate([real_part, imag_part], axis=-1).astype(jnp.bfloat16)
    products = products.reshape(TRANSFERS, kpoints, local_aux, OCCUPIED_BANDS, doubled)
    gathered = lax.all_gather(products, "aux", axis=2, tiled=True)
    stacked = jnp.concatenate([gathered, rotated_parts(gathered, band_count)], axis=2)
    stacked = stacked.reshape(TRANSFERS, kpoints, 2 * NAUX, OCCUPIED_BANDS * doubled)
    screened = jnp.stack(
        [
            jnp.einsum(
                "ab,kbx->kax",
                screens[momentum_transfer],
                stacked[momentum_transfer],
                preferred_element_type=jnp.float32,
            )
            for momentum_transfer in range(TRANSFERS)
        ]
    ).astype(jnp.bfloat16)
    left_side = products.reshape(TRANSFERS, kpoints, local_aux * OCCUPIED_BANDS, doubled)
    right_side = screened.reshape(TRANSFERS, kpoints, local_aux * OCCUPIED_BANDS, doubled)
    blocks = jnp.einsum("tkxm,tkxn->kmn", left_side, right_side, preferred_element_type=jnp.float32)
    sigma_real, sigma_imag = sigma_parts(blocks, band_count)
    local_sigma = prefactor * jnp.concatenate([sigma_real, sigma_imag], axis=-1)
    return lax.psum_scatter(
        local_sigma.astype(jnp.bfloat16), "aux", scatter_dimension=1, tiled=True
    ).astype(jnp.float32)


def solution(mesh):
    in_specs = (
        P("ka", None, None),
        P("aux", None, None, None),
        P("aux", None),
        P("ka", "aux", None),
        P(),
        P(),
    )
    out_specs = P("ka", "aux", None)
    return jax.shard_map(local, mesh=mesh, in_specs=in_specs, out_specs=out_specs, check_vma=False)
```

profile of v0, /device:TPU:1, one launch (start us, length us, event | category | flops | bytes accessed | tf_op | source)
XLA Modules:
  0.0 1266.1 jit_solution(11073490766987483804)
XLA Ops:
  7.4 2.0 fusion.51
  9.4 0.3 copy.66
  9.7 0.3 copy.67
  10.0 0.5 copy.45
  10.5 0.6 reshape.199
  11.1 0.5 broadcast.52
  11.7 2.2 reduce
  13.9 0.0 copy-start.5
  13.9 0.8 reshape.201
  14.7 15.0 %all-to-all-start = ((bf16[128,2,512]{2,1,0:T(2,128)(2,1)}), bf16[128,2,512]{2,1,0:T(2,128)(2,1)S(1)}, u32[]{:S(2)}, u32[]{:S(2)}) async-start(bf16[128,2,512]{2,1,0:T(2,128)(2,1)} %reshape.201), calls=%async_computation | async-start | bytes 524288 | tf_op jit(solution)/shard_map/all_to_all | solution.py:50
  29.7 14.4 %all-to-all-done = bf16[128,2,512]{2,1,0:T(2,128)(2,1)S(1)} async-done(((bf16[128,2,512]{2,1,0:T(2,128)(2,1)}), bf16[128,2,512]{2,1,0:T(2,128)(2,1)S(1)}, u32[]{:S(2)}, u32[]{:S(2)}) %all-to-all-start) | async-done | bytes 262176 | tf_op jit(solution)/shard_map/all_to_all | solution.py:50
  44.1 0.2 reshape.202
  44.4 0.8 gather_fusion
  45.2 0.3 broadcast_select_fusion
  45.6 0.8 slice_bitcast_fusion.1
  46.4 5.5 all-to-all-start.2
  51.9 0.1 copy.42
  52.0 14.5 %all-to-all-done.2 = bf16[128,8,128]{2,1,0:T(8,128)(2,1)S(1)} async-done(((bf16[128,8,128]{2,1,0:T(8,128)(2,1)}), bf16[128,8,128]{2,1,0:T(8,128)(2,1)S(1)}, u32[]{:S(2)}, u32[]{:S(2)}) %all-to-all-start.2) | async-done | bytes 262176 | tf_op jit(solution)/shard_map/all_to_all | solution.py:54
  66.5 5.4 all-to-all-start.1
  71.9 0.5 all-gather.2.cloned.1.call-start
  72.4 0.1 copy.47
  72.5 0.1 reshape.184
  72.6 0.9 constant_dynamic-slice_fusion
  73.5 0.4 stack.19
  73.9 12.5 all-to-all-done.1
  86.5 1.4 stack.18
  87.9 1.7 maximum_bitcast_fusion
  89.6 2.1 gather_fusion.1
  91.7 2.7 copy.48
  94.4 4.8 fusion.15
  99.3 7.1 reshape.200
  106.4 5.1 fusion.12
  111.5 4.6 fusion.7
  116.1 2.5 copy.52
  118.6 0.6 copy.53
  119.2 0.0 copy-start.1
  119.3 1.7 copy-done.1
  120.9 3.4 pad_maximum_fusion
  124.3 0.0 all-gather.2.cloned.1.call-update
  124.4 0.0 all-reduce.3.cloned.1.call-start
  124.4 0.6 copy-done.3
  125.0 0.6 fusion.52
  126.9 2.8 select_bitcast_fusion.1
  129.7 0.0 all-reduce.3.cloned.1.call-update
  129.7 0.2 reduce-scatter.2.cloned.1.call-start
  129.9 2.5 copy.54
  132.4 4.6 copy.55
  137.0 70.2 %all-gather.2.cloned.1.call-done = bf16[2,1,768,16,128]{4,3,2,0,1:T(8,128)(2,1)} async-done(((bf16[2,1,384,16,128]{4,3,2,0,1:T(8,128)(2,1)}), bf16[2,1,768,16,128]{4,3,2,0,1:T(8,128)(2,1)}) %all-gather.2.cloned.1.call-update) | async-done | bytes 6291472 | tf_op jit(solution)/shard_map/all_gather | solution.py:88
  207.3 6.6 slice_negate_fusion
  213.9 34.4 %maximum_maximum_fusion = bf16[2,1,1536,16,128]{4,3,2,0,1:T(8,128)(2,1)S(1)} fusion(bf16[2,1,768,16,64]{4,3,2,0,1:T(8,128)(2,1)S(1)} %get-tuple-element.12, bf16[2,1,768,16,64]{4,3,2,0,1:T(8,128)(2,1)S(1)} %get-tuple-element.11, bf16[2,1,768,16,128]{4,3,2,0,1:T(8,128)(2,1)S(1)} %copy-done), kind=kLoop, calls=%fused_computation.2 | loop fusion | flops 37748736 | bytes 25165824 | tf_op jit(solution)/shard_map/concatenate | solution.py:89
  248.2 5.6 fusion.50
  253.9 962.7 %all-reduce.3.cloned.1.call-done = (bf16[384,1536]{1,0:T(8,128)(2,1)}, bf16[384,1536]{1,0:T(8,128)(2,1)}) async-done(((bf16[384,1536]{1,0:T(8,128)(2,1)}, bf16[384,1536]{1,0:T(8,128)(2,1)}), (bf16[384,1536]{1,0:T(8,128)(2,1)}, bf16[384,1536]{1,0:T(8,128)(2,1)})) %all-reduce.3.cloned.1.call-update) | async-done | bytes 2359312 | tf_op jit(solution)/shard_map/psum | solution.py:18
  1216.6 7.1 fusion.32
  1223.7 0.8 copy.58
  1224.5 0.8 stack.21
  1225.3 8.3 fusion.29
  1233.6 1.7 copy.59
  1235.3 2.1 stack.22
  1237.4 3.3 fusion.37
  1240.7 0.1 slice_add_fusion.1
  1240.8 0.7 fusion.46
  1241.5 0.0 reduce-scatter.2.cloned.1.call-update
  1241.5 15.6 %reduce-scatter.2.cloned.1.call-done = bf16[1,32,128]{2,1,0:T(8,128)(2,1)} async-done(((bf16[1,64,128]{2,1,0:T(8,128)(2,1)}), bf16[1,32,128]{2,1,0:T(8,128)(2,1)}) %reduce-scatter.2.cloned.1.call-update) | async-done | bytes 8208 | tf_op jit(solution)/shard_map/reduce_scatter | solution.py:107
  1257.2 1.3 convert_element_type.46
  (16 shorter events, 0.1 us)
Async XLA Ops:
  9.7 20.0 %copy-start.4 = (s32[2,128]{1,0:T(2,128)S(1)}, s32[2,128]{1,0:T(2,128)}, u32[]{:S(2)}) copy-start(s32[2,128]{1,0:T(2,128)} %param.10) | copy-start | bytes 3076
  13.9 38.0 %copy-start.5 = (s32[32,2]{0,1:T(2,128)S(1)}, s32[32,2]{0,1:T(2,128)}, u32[]{:S(2)}) copy-start(s32[32,2]{0,1:T(2,128)} %param.8) | copy-start | bytes 772
  14.7 57.9 %copy-start.2 = (bf16[1,4096,128]{2,1,0:T(8,128)(2,1)S(1)}, bf16[1,4096,128]{2,1,0:T(8,128)(2,1)}, u32[]{:S(2)}) copy-start(bf16[1,4096,128]{2,1,0:T(8,128)(2,1)} %param.6) | copy-start | bytes 3145732
  14.7 29.4 %all-to-all-start = ((bf16[128,2,512]{2,1,0:T(2,128)(2,1)}), bf16[128,2,512]{2,1,0:T(2,128)(2,1)S(1)}, u32[]{:S(2)}, u32[]{:S(2)}) async-start(bf16[128,2,512]{2,1,0:T(2,128)(2,1)} %reshape.201), calls=%async_computation | async-start | bytes 524288 | tf_op jit(solution)/shard_map/all_to_all | solution.py:50
  46.4 20.1 %all-to-all-start.2 = ((bf16[128,8,128]{2,1,0:T(8,128)(2,1)}), bf16[128,8,128]{2,1,0:T(8,128)(2,1)S(1)}, u32[]{:S(2)}, u32[]{:S(2)}) async-start(bf16[128,8,128]{2,1,0:T(8,128)(2,1)} %get-tuple-element.18), calls=%async_computation.2 | async-start | bytes 524288 | tf_op jit(solution)/shard_map/all_to_all | solution.py:54
  66.5 20.0 %all-to-all-start.1 = ((bf16[128,8,128]{2,1,0:T(8,128)(2,1)}), bf16[128,8,128]{2,1,0:T(8,128)(2,1)S(1)}, u32[]{:S(2)}, u32[]{:S(2)}) async-start(bf16[128,8,128]{2,1,0:T(8,128)(2,1)} %get-tuple-element.17), calls=%async_computation.1 | async-start | bytes 524288 | tf_op jit(solution)/shard_map/all_to_all | solution.py:54
  71.9 135.4 %all-gather.2.cloned.1.call-start = ((), (), s32[]{:S(2)}) async-start(), calls=%async_computation.4 | async-start | bytes 9437184 | tf_op jit(solution)/shard_map/all_gather | solution.py:88
  119.2 1.7 copy-start.1
  124.3 0.7 copy-start.3
  124.4 1092.2 %all-reduce.3.cloned.1.call-start = ((), (), s32[]{:S(2)}) async-start(), calls=%async_computation.6 | async-start | bytes 4718592 | tf_op jit(solution)/shard_map/psum | solution.py:18
  129.7 1127.4 %reduce-scatter.2.cloned.1.call-start = ((), (), s32[]{:S(2)}) async-start(), calls=%async_computation.5 | async-start | bytes 24576 | tf_op jit(solution)/shard_map/reduce_scatter | solution.py:107
  207.2 6.6 copy-start
Sparse Core Ops, SparseCore 0:
  124.5 82.7 all-gather.1
  1241.6 15.4 reduce-scatter.1
Sparse Core Ops, SparseCore 1:
  129.8 1086.7 all-reduce.2
where the time goes:
time: 1270 us
  waiting for transfers between devices  1090 us (86%)
  other arithmetic  58.1 us (5%)
  local copies, waits for them, and re-layouts  46 us (4%)
  matrix products  28.7 us (2%)
  starting transfers between devices  26.6 us (2%)
  between operations  16.7 us (1%)
    psum x1, waiting for transfers between devices, from_root(): return lax.psum(block, axis)  963 us
    all_gather x1, waiting for transfers between devices, local(): gathered = lax.all_gather(products, 'aux', axis=2, tiled=True)  70.2 us
    concatenate x1, other arithmetic, local(): jnp.concatenate([gathered, rotated_parts(gathered, band_count)], axis=2)  34.4 us
    all_to_all x2, waiting for transfers between devices, local(): lax.all_to_all(permuted[momentum_transfer], 'ka', split_axis=0, concat_ax...  27 us
  transfers between devices with their start and end apart: 6, of which 6 were waited for; matrix products, arithmetic and copies ran while one was open for 5% of the time, Pallas kernels for 0%

commit v1 on v0

v1 whole, which is shorter than its diff:
```python
import math

import jax
import jax.numpy as jnp
from jax import lax
from jax.experimental import pallas as pl
from jax.experimental.pallas import tpu as pltpu
from jax.sharding import Mesh
from jax.sharding import PartitionSpec as P

ATOMS = 64
ORBS = 64
AUX_ATOM = 12
BANDS = 64
OCC = 16
TRANSFERS = 2
NAUX = ATOMS * AUX_ATOM
HALF = NAUX // 2
BF = jnp.bfloat16
F32 = jnp.float32
KA = ("z", "xl", "y", "core")
PEERS = 128
FAR_TILES = 64
W_TILES = HALF * NAUX // (16 * 128)
PREFACTOR = -1.0 / math.sqrt(TRANSFERS * NAUX * OCC)
VMEM = 56 * 2**20


def dot(a, b):
    return jnp.dot(a, b, preferred_element_type=F32)


def w_slot(w):
    return (w, 16) if w < PEERS else (FAR_TILES + w - PEERS, 0)


def pack_kernel(h_ref, c_ref, w_ref, out_ref):
    y = lax.broadcasted_iota(jnp.int32, (2 * OCC, 128), 0)
    col = lax.broadcasted_iota(jnp.int32, (2 * OCC, 128), 1)
    pick = (col == jnp.where(y < OCC, y, y + BANDS - OCC)).astype(F32).astype(BF)
    for ob in range(FAR_TILES // 2):
        far = lax.dot_general(
            pick,
            c_ref[ob * 128 : (ob + 1) * 128, :],
            (((1,), (1,)), ((), ())),
            preferred_element_type=F32,
        ).astype(BF)
        out_ref[2 * ob, 0:16, :] = far[0:16]
        out_ref[2 * ob + 1, 0:16, :] = far[16:32]
    row0 = h_ref[0] * HALF
    r16 = lax.broadcasted_iota(jnp.int32, (16, 128), 0)
    c16 = lax.broadcasted_iota(jnp.int32, (16, 128), 1)
    for rb in range(HALF // 16):
        for cb in range(NAUX // 128):
            above = (c16 + cb * 128) - (r16 + rb * 16) - row0
            rows = slice(rb * 16, rb * 16 + 16)
            wr = w_ref[rows, cb * 128 : cb * 128 + 128].astype(F32)
            wi = w_ref[rows, NAUX + cb * 128 : NAUX + cb * 128 + 128].astype(F32)
            packed = jnp.where(above > 0, wr, jnp.where(above == 0, 0.5 * wr, wi))
            j, at = w_slot(rb * (NAUX // 128) + cb)
            out_ref[j, at : at + 16, :] = packed.astype(BF)
    for j in range(FAR_TILES + W_TILES - PEERS, PEERS):
        out_ref[j, 0:16, :] = jnp.zeros((16, 128), BF)


def route_kernel(s_ref, partner_ref, r_ref, own_ref, got_ref, out_ref):
    first = s_ref[0] == 0
    is_far = s_ref[1] < FAR_TILES
    own, got = own_ref[0].astype(F32), got_ref[0].astype(F32)
    halves = (
        jnp.where(first, own, got).astype(BF),
        jnp.where(first, got, own).astype(BF),
    )
    for k in range(PEERS):
        out_ref[k, 16:32, :] = halves[k % 2][16:32]

    @pl.when(is_far)
    def _():
        for k in range(PEERS):
            out_ref[k, 0:16, :] = r_ref[partner_ref[k], 0:16, :]

    @pl.when(jnp.logical_not(is_far))
    def _():
        for k in range(PEERS):
            out_ref[k, 0:16, :] = halves[k % 2][0:16]


GROUP = 4
STEPS = ATOMS // GROUP


def pair_kernel(h_ref, nbr_ref, far_ref, own_ref, oth_ref, c_ref, out_ref, x_ref, w_ref, p_ref):
    step = pl.program_id(0)
    h = h_ref[0]
    low32 = lax.broadcasted_iota(jnp.int32, (2 * OCC, 128), 1) < ORBS

    @pl.when(step == 0)
    def _():
        for ob in range(FAR_TILES // 2):
            both = jnp.concatenate(
                [far_ref[2 * ob, 0:16, :], far_ref[2 * ob + 1, 0:16, :]], axis=0
            ).astype(F32)
            turned = pltpu.roll(both, 64, 1)
            x_ref[2 * ob] = jnp.where(low32, both, turned).astype(BF)
            x_ref[2 * ob + 1] = jnp.where(low32, turned, both).astype(BF)
        w_ref[...] = jnp.zeros_like(w_ref)

    def group(triple_ref, half):
        for g in range(GROUP):
            at = step * GROUP + g
            n0 = nbr_ref[at, 0]
            n1 = nbr_ref[at, 1]
            lhs = jnp.where(
                low32, x_ref[n0].astype(F32), x_ref[n1].astype(F32)
            ).astype(BF)
            pair = dot(lhs, triple_ref[g]).astype(BF)
            atom = half * (ATOMS // 2) + lax.rem(at, ATOMS // 2)
            own = c_ref[pl.ds(pl.multiple_of(atom * ORBS, ORBS), ORBS), :].astype(F32)
            sign = jnp.where(lax.broadcasted_iota(jnp.int32, own.shape, 1) < BANDS, 1.0, -1.0)
            first = (own * sign).astype(BF)
            second = pltpu.roll(own, BANDS, 1).astype(BF)
            w_ref[g, 0:64, 0:128] = first
            w_ref[g, 64:128, 128:256] = first
            w_ref[g, 128:192, 0:128] = second
            w_ref[g, 192:256, 128:256] = second
            left = jnp.concatenate(
                [
                    jnp.concatenate(
                        [pair[0:16, q * 128 : q * 128 + 128], pair[16:32, q * 128 : q * 128 + 128]],
                        axis=1,
                    )
                    for q in range(AUX_ATOM // 2)
                ],
                axis=0,
            )
            prod = dot(left, w_ref[g])
            for q in range(AUX_ATOM // 2):
                for e in range(2):
                    mu = atom * AUX_ATOM + 2 * q + e
                    for s in range(2):
                        p_ref[pl.ds(mu + s * 8 * NAUX, 8, stride=NAUX), :] = prod[
                            q * 16 + s * 8 : q * 16 + s * 8 + 8, e * 128 : e * 128 + 128
                        ]

    @pl.when(step < STEPS // 2)
    def _():
        group(own_ref, h)

    @pl.when(step >= STEPS // 2)
    def _():
        group(oth_ref, 1 - h)

    @pl.when(step == STEPS - 1)
    def _():
        for l in range(OCC):
            out_ref[l] = p_ref[l * NAUX : (l + 1) * NAUX, :].astype(BF)


BLK = 256
NB = NAUX // BLK


def sigma_kernel(s_ref, p_ref, wa_ref, wb_ref, keep_ref, send_ref, a_ref, b_ref, acc_ref, sig_ref):
    pair = pl.program_id(0)

    @pl.when(pair == 0)
    def _():
        core0 = s_ref[1] == 0
        r16 = lax.broadcasted_iota(jnp.int32, (16, 128), 0)
        c16 = lax.broadcasted_iota(jnp.int32, (16, 128), 1)
        for half in range(2):
            for rb in range(HALF // 16):
                row = half * HALF + rb * 16
                blk, at = row // BLK, row % BLK
                for cb in range(NAUX // 128):
                    j, base = w_slot(rb * (NAUX // 128) + cb)
                    va = wa_ref[j, base : base + 16, :].astype(F32)
                    vb = wb_ref[j, base : base + 16, :].astype(F32)
                    tile = jnp.where(core0, va, vb) if half == 0 else jnp.where(core0, vb, va)
                    cblk, cat = cb * 128 // BLK, cb * 128 % BLK
                    above = (c16 + cb * 128) - (r16 + row)
                    if cblk >= blk:
                        lo = (cblk - blk) * BLK + cat
                        up = tile if cblk > blk else jnp.where(above >= 0, tile, 0.0)
                        a_ref[blk, at : at + 16, lo : lo + 128] = up.astype(BF)
                    if cblk <= blk:
                        lo = (NB - blk + cblk) * BLK + cat
                        down = tile if cblk < blk else jnp.where(above < 0, tile, 0.0)
                        a_ref[blk, at : at + 16, lo : lo + 128] = down.astype(BF)
        acc_ref[...] = jnp.zeros_like(acc_ref)

    low = lax.broadcasted_iota(jnp.int32, (NAUX, 128), 1) < BANDS
    for s in range(2):
        val = p_ref[s]
        b_ref[0:NAUX, s * 128 : s * 128 + 128] = val
        turned = pltpu.roll(val.astype(F32), BANDS, 1)
        b_ref[NAUX : 2 * NAUX, s * 128 : s * 128 + 128] = jnp.where(low, -turned, turned).astype(BF)
    for blk in range(NB):
        scr = dot(a_ref[blk], b_ref[blk * BLK : blk * BLK + (NB + 1) * BLK, :]).astype(BF)
        for s in range(2):
            acc_ref[...] += lax.dot_general(
                p_ref[s, blk * BLK : blk * BLK + BLK, :],
                scr[:, s * 128 : s * 128 + 128],
                (((0,), (0,)), ((), ())),
                preferred_element_type=F32,
            )

    @pl.when(pair == pl.num_programs(0) - 1)
    def _():
        y = acc_ref[...]
        z = y + y.T
        re = z[:BANDS, :BANDS] + z[BANDS:, BANDS:]
        im = z[:BANDS, BANDS:] - z[BANDS:, :BANDS]
        sig_ref[...] = PREFACTOR * jnp.concatenate([re, im], axis=1)
        h = s_ref[0]
        rows = BANDS // 2
        keep_ref[...] = sig_ref[pl.ds(pl.multiple_of(h * rows, rows), rows), :]
        send_ref[...] = sig_ref[pl.ds(pl.multiple_of((1 - h) * rows, rows), rows), :]


def params():
    return pltpu.CompilerParams(vmem_limit_bytes=VMEM)


def whole(shape):
    return pl.BlockSpec(shape, lambda i, *_: (0,) * len(shape))


def local(coefficients, triple, neighbors, w_screened, partner, q_ids):
    h = lax.axis_index("aux").astype(jnp.int32)
    me = lax.axis_index(KA).astype(jnp.int32)
    core = lax.axis_index("core").astype(jnp.int32)
    swap = [(0, 1), (1, 0)]
    atoms = triple.shape[0]
    coef = coefficients[0]
    triple = triple.reshape(atoms, 2 * ORBS, AUX_ATOM * ORBS)

    share = atoms // 8
    mine = lax.axis_index(("y", "core")) * share
    crossed = lax.ppermute(lax.dynamic_slice_in_dim(triple, mine, share, 0), "aux", swap)
    nbr_other = lax.ppermute(neighbors, "aux", swap)
    nbr = jnp.concatenate([neighbors, nbr_other], axis=0)

    smem = pl.BlockSpec(memory_space=pltpu.SMEM)
    vmem = pl.BlockSpec(memory_space=pltpu.VMEM)
    piece = jax.ShapeDtypeStruct((PEERS, 32, 128), BF)
    packed = pl.pallas_call(
        pack_kernel,
        out_shape=piece,
        in_specs=[smem, vmem, vmem],
        out_specs=vmem,
        compiler_params=params(),
        name="pack",
    )(h[None], coef, w_screened[0])
    spread = lax.all_to_all(packed, KA, split_axis=0, concat_axis=0, tiled=True)

    crossed, spread = lax.optimization_barrier((crossed, spread))
    other = lax.all_gather(crossed, ("y", "core"), axis=0, tiled=True)

    own_tile = lax.dynamic_slice_in_dim(spread, q_ids[h], 1, 0)
    got_tile = lax.ppermute(
        lax.dynamic_slice_in_dim(spread, q_ids[1 - h], 1, 0), "aux", swap
    )
    partner_here = lax.dynamic_slice_in_dim(partner, h, 1, 0)[0]
    routed = pl.pallas_call(
        route_kernel,
        out_shape=piece,
        in_specs=[smem, smem, vmem, vmem, vmem],
        out_specs=vmem,
        compiler_params=params(),
        name="route",
    )(jnp.stack([h, me]), partner_here, spread, own_tile, got_tile)
    arrived = lax.all_to_all(routed, KA, split_axis=0, concat_axis=0, tiled=True)
    arrived2 = lax.ppermute(arrived, "core", swap)

    half_steps = STEPS // 2
    products = pl.pallas_call(
        pair_kernel,
        out_shape=jax.ShapeDtypeStruct((OCC, NAUX, 128), BF),
        grid=(STEPS,),
        in_specs=[
            smem,
            smem,
            whole((PEERS, 32, 128)),
            pl.BlockSpec(
                (GROUP, 2 * ORBS, AUX_ATOM * ORBS),
                lambda i: (jnp.minimum(i, half_steps - 1), 0, 0),
            ),
            pl.BlockSpec(
                (GROUP, 2 * ORBS, AUX_ATOM * ORBS),
                lambda i: (jnp.maximum(i - half_steps, 0), 0, 0),
            ),
            whole((ATOMS * ORBS, 128)),
        ],
        out_specs=whole((OCC, NAUX, 128)),
        scratch_shapes=[
            pltpu.VMEM((ATOMS, 2 * OCC, 128), BF),
            pltpu.VMEM((GROUP, 256, 256), BF),
            pltpu.VMEM((OCC * NAUX, 128), F32),
        ],
        compiler_params=params(),
        cost_estimate=pl.CostEstimate(flops=4_000_000_000, bytes_accessed=17_000_000, transcendentals=0),
        name="pair_products",
    )(h[None], nbr, arrived, triple, other, coef)

    rows = BANDS // 2
    part = jax.ShapeDtypeStruct((rows, 2 * BANDS), F32)
    keep, send = pl.pallas_call(
        sigma_kernel,
        out_shape=(part, part),
        grid=(OCC // 2,),
        in_specs=[
            smem,
            pl.BlockSpec((2, NAUX, 128), lambda i: (i, 0, 0)),
            whole((PEERS, 32, 128)),
            whole((PEERS, 32, 128)),
        ],
        out_specs=(whole((rows, 2 * BANDS)),) * 2,
        scratch_shapes=[
            pltpu.VMEM((NB, BLK, (NB + 1) * BLK), BF),
            pltpu.VMEM((2 * NAUX, 256), BF),
            pltpu.VMEM((128, 128), F32),
            pltpu.VMEM((BANDS, 128), F32),
        ],
        compiler_params=params(),
        name="screened_sigma",
    )(jnp.stack([h, core]), products, arrived, arrived2)
    return (keep + lax.ppermute(send, "aux", swap))[None]


def solution(mesh):
    ka, aux = mesh.devices.shape
    fine = Mesh(mesh.devices.reshape(8, 2, 4, 2, aux), (*KA, "aux"))
    in_specs = (
        P(KA, None, None),
        P("aux", None, None, None),
        P("aux", None),
        P(KA, "aux", None),
        P(),
        P(),
    )
    return jax.shard_map(
        local, mesh=fine, in_specs=in_specs, out_specs=P(KA, "aux", None), check_vma=False
    )
```

time: 1270 us -> 167 us (0.13)
  waiting for transfers between devices: 1090 us -> 32.5 us
  other arithmetic: 58.1 us -> 2.65 us
  blocking collectives: 0 us -> 42 us
  local copies, waits for them, and re-layouts: 46 us -> 6.24 us
  Pallas kernels: 0 us -> 39 us
  matrix products: 28.7 us -> 0 us
    psum x1 -> x0, waiting for transfers between devices: 963 us -> none  [from_root(): return lax.psum(block, axis)]
    all_gather x1, waiting for transfers between devices: 70.2 us -> 0.01 us  [local(): other = lax.all_gather(crossed, ('y', 'core'), axis=0, tiled=True)]
    all_to_all x0 -> x1, blocking collectives: none -> 42 us  [local(): lax.all_to_all(routed, KA, split_axis=0, concat_axis=0, tiled=True)]
    all_to_all x3 -> x1, waiting for transfers between devices: 41.4 us -> 0.01 us  [local(): spread = lax.all_to_all(packed, KA, split_axis=0, concat_axis=0, tiled=True)]
    pallas_call x0 -> x4, Pallas kernels: none -> 39 us  [the longest x1 19.7 us: local(): pl.pallas_call(pair_kernel, out_shape=jax.ShapeDtypeStruct((OCC, NAUX, 12...]
    concatenate x3 -> x1, other arithmetic: 37.8 us -> 0.07 us  [local(): nbr = jnp.concatenate([neighbors, nbr_other], axis=0)]
    ppermute x0 -> x5, waiting for transfers between devices: none -> 32.5 us  [the longest x1 27.3 us: local(): lax.ppermute(lax.dynamic_slice_in_dim(triple, mine, share, 0), 'aux', swap)]
    dot_general x5 -> x0, matrix products: 28.7 us -> none  [the longest x2 15.4 us: local(): jnp.einsum('ab,kbx->kax', screens[momentum_transfer], stacked[momentum_tr...]
  transfers between devices with their start and end apart: 6 -> 7, of which waited for: 6 -> 4; matrix products, arithmetic and copies ran while one was open for 5% -> 3% of each run, Pallas kernels for 0% -> 14%
where the time goes in v1:
time: 167 us; the launch traced here: 164 us
  blocking collectives  42 us (25%)
  Pallas kernels  39 us (23%)
  waiting for transfers between devices  32.5 us (19%)
  starting transfers between devices  24.3 us (15%)
  between operations  17.4 us (10%)
  local copies, waits for them, and re-layouts  6.24 us (4%)
  other arithmetic  2.65 us (2%)
    all_to_all x1, blocking collectives, local(): lax.all_to_all(routed, KA, split_axis=0, concat_axis=0, tiled=True)  42 us
    ppermute x1, waiting for transfers between devices, local(): lax.ppermute(lax.dynamic_slice_in_dim(triple, mine, share, 0), 'aux', swap)  27.3 us
    pallas_call x1, Pallas kernels, local(): pl.pallas_call(pair_kernel, out_shape=jax.ShapeDtypeStruct((OCC, NAUX, 12...  19.7 us
    all_to_all x1, starting transfers between devices, local(): spread = lax.all_to_all(packed, KA, split_axis=0, concat_axis=0, tiled=True)  14.9 us
    pallas_call x1, Pallas kernels, local(): pl.pallas_call(sigma_kernel, out_shape=(part, part), grid=(OCC // 2,), in...  13.3 us
    pallas_call x1, Pallas kernels, local(): pl.pallas_call(pack_kernel, out_shape=piece, in_specs=[smem, vmem, vmem],...  3.57 us
  transfers between devices with their start and end apart: 7, of which 4 were waited for; matrix products, arithmetic and copies ran while one was open for 3% of the time, Pallas kernels for 14%

profile of v1, /device:TPU:1, one launch (start us, length us, event | category | flops | bytes accessed | tf_op | source)
XLA Modules:
  0.0 164.1 jit_solution(10400926649653147358)
XLA Ops:
  6.5 0.0 copy-start
  6.5 0.0 copy-start.6
  6.5 0.0 copy-start.7
  6.5 3.6 %pack.1 = bf16[128,32,128]{2,1,0:T(8,128)(2,1)} custom-call(s32[1]{0:T(128)} %bitcast.h_ref, bf16[4096,128]{1,0:T(8,128)(2,1)} %bitcast.14, bf16[384,1536]{1,0:T(8,128)(2,1)} %bitcast.16), custom_call_target="tpu_custom_call" | custom-call | tf_op jit(solution)/shard_map/pack/pallas_call | solution.py:247
  10.1 14.9 %all-to-all-start = ((bf16[128,32,128]{2,1,0:T(8,128)(2,1)}), bf16[128,32,128]{2,1,0:T(8,128)(2,1)S(1)}, u32[]{:S(2)}, u32[]{:S(2)}) async-start(bf16[128,32,128]{2,1,0:T(8,128)(2,1)} %pack.1), calls=%async_computation | async-start | bytes 2097152 | tf_op jit(solution)/shard_map/all_to_all | solution.py:255
  25.0 0.0 all-gather.2.cloned.1.call-start
  25.0 1.2 constant_dynamic-slice_fusion.2
  26.2 2.5 %collective-permute-start.1 = (bf16[4,128,768]{2,1,0:T(8,128)(2,1)S(1)}, bf16[4,128,768]{2,1,0:T(8,128)(2,1)S(1)}, u32[]{:S(2)}, u32[]{:S(2)}) collective-permute-start(bf16[4,128,768]{2,1,0:T(8,128)(2,1)S(1)} %constant_dynamic-slice_fusion.2), channel_id=1, source_target_pairs={{0,1},{1,0},{2,3},{3,2},{4,5},{5,4},{6,7},{7,6},{8,9},{9,8},{10,11... | collective-permute-start | bytes 2359304 | tf_op jit(solution)/shard_map/ppermute | solution.py:240
  28.8 27.3 %collective-permute-done.1 = bf16[4,128,768]{2,1,0:T(8,128)(2,1)S(1)} collective-permute-done((bf16[4,128,768]{2,1,0:T(8,128)(2,1)S(1)}, bf16[4,128,768]{2,1,0:T(8,128)(2,1)S(1)}, u32[]{:S(2)}, u32[]{:S(2)}) %collective-permute-start.1) | collective-permute-done | bytes 786464 | tf_op jit(solution)/shard_map/ppermute | solution.py:240
  56.1 0.0 copy-start.4
  56.1 0.0 all-to-all-done.r_ref
  56.1 0.0 copy-start.2
  56.1 1.0 copy-done.4
  57.1 0.0 all-gather.2.cloned.1.call-update
  57.1 0.0 copy-done.6
  57.1 0.7 fusion.1
  61.8 0.7 pad_add_fusion.2.s_ref
  62.4 0.6 constant_dynamic-slice_fusion
  63.0 1.9 %collective-permute-start.2 = (bf16[1,32,128]{2,1,0:T(8,128)(2,1)S(1)}, bf16[1,32,128]{2,1,0:T(8,128)(2,1)S(1)}, u32[]{:S(2)}, u32[]{:S(2)}) collective-permute-start(bf16[1,32,128]{2,1,0:T(8,128)(2,1)S(1)} %get-tuple-element.13), channel_id=1, source_target_pairs={{0,1},{1,0},{2,3},{3,2},{4,5},{5,4},{6,7},{7,6},{8,9},{9,8},{10,11... | collective-permute-start | bytes 24584 | tf_op jit(solution)/shard_map/ppermute | solution.py:261
  64.9 0.0 copy-done
  64.9 0.5 fusion.partner_ref
  65.5 1.6 collective-permute-done.2.got_ref
  67.0 0.0 copy-start.5
  67.0 0.0 copy-done.2
  67.0 0.6 copy-done.5
  67.6 2.5 %route.1 = bf16[128,32,128]{2,1,0:T(8,128)(2,1)} custom-call(s32[2]{0:T(128)} %pad_add_fusion.2.s_ref, s32[128]{0:T(128)} %fusion.partner_ref, bf16[128,32,128]{2,1,0:T(8,128)(2,1)} %copy-done.2, bf16[1,32,128]{2,1,0:T(8,128)(2,1)} %get-tuple-element.14.own_ref, bf16[1,32,128]{2,1,0:T(8,128)(2,1)} %copy-done.5), custom_call_target="tpu_custom_call" | custom-call | tf_op jit(solution)/shard_map/route/pallas_call | solution.py:265
  70.1 42.0 %all_to_all.10.far_ref.wa_ref = bf16[128,32,128]{2,1,0:T(8,128)(2,1)S(1)} all-to-all(bf16[128,32,128]{2,1,0:T(8,128)(2,1)} %route.1), channel_id=1, replica_groups=mesh['z'=8,'xl'=2,'y'=4,'core'=2,'aux'=2] {'z','xl','y','core'}, dimensions={0} | all-to-all | bytes 2097152 | tf_op jit(solution)/shard_map/all_to_all | solution.py:273
  112.1 0.0 copy-start.1
  112.1 0.8 collective-permute-start.3
  112.9 0.0 copy-done.7
  112.9 2.1 %collective-permute-start = (s32[32,2]{0,1:T(2,128)S(1)}, s32[32,2]{0,1:T(2,128)S(1)}, u32[]{:S(2)}, u32[]{:S(2)}) collective-permute-start(s32[32,2]{0,1:T(2,128)S(1)} %copy-done.7), channel_id=1, source_target_pairs={{0,1},{1,0},{2,3},{3,2},{4,5},{5,4},{6,7},{7,6},{8,9},{9,8},{10,11... | collective-permute-start | bytes 776 | tf_op jit(solution)/shard_map/ppermute | solution.py:241
  115.0 0.6 pad_add_fusion.1.s_ref
  115.6 1.3 collective-permute-done
  116.9 0.1 pad_add_fusion
  117.0 0.7 copy.9.nbr_ref
  117.7 0.0 all-gather.2.cloned.1.call-done.oth_ref
  117.7 0.0 copy-done.1
  117.7 19.7 %pair_products.1.p_ref = bf16[16,768,128]{2,1,0:T(8,128)(2,1)} custom-call(s32[1]{0:T(128)} %bitcast.h_ref, s32[64,2]{1,0:T(8,128)} %copy.9.nbr_ref, bf16[128,32,128]{2,1,0:T(8,128)(2,1)} %copy-done.1, bf16[32,128,768]{2,1,0:T(8,128)(2,1)} %bitcast.13, bf16[32,128,768]{2,1,0:T(8,128)(2,1)} %all-gather.2.cloned.1.call-done.oth_ref, bf16[4096,128]{1,0:T(8,128)(2,1)} %bitcast.15), custom_call_target="tpu_custom_call" | custom-call | flops 4000000000 | bytes 17000000 | tf_op jit(solution)/shard_map/pair_products/pallas_call | solution.py:277
  137.4 0.0 collective-permute-done.3.wb_ref
  137.4 0.0 copy-start.3
  137.4 1.0 copy-done.3
  138.4 13.3 %screened_sigma.1 = (f32[32,128]{1,0:T(8,128)}, f32[32,128]{1,0:T(8,128)}) custom-call(s32[2]{0:T(128)} %pad_add_fusion.1.s_ref, bf16[16,768,128]{2,1,0:T(8,128)(2,1)} %pair_products.1.p_ref, bf16[128,32,128]{2,1,0:T(8,128)(2,1)} %copy-done.1, bf16[128,32,128]{2,1,0:T(8,128)(2,1)} %copy-done.3), custom_call_target="tpu_custom_call" | custom-call | tf_op jit(solution)/shard_map/screened_sigma/pallas_call | solution.py:308
  151.7 2.1 %collective-permute-start.4 = (f32[32,128]{1,0:T(8,128)}, f32[32,128]{1,0:T(8,128)S(1)}, u32[]{:S(2)}, u32[]{:S(2)}) collective-permute-start(f32[32,128]{1,0:T(8,128)} %get-tuple-element.12), channel_id=1, source_target_pairs={{0,1},{1,0},{2,3},{3,2},{4,5},{5,4},{6,7},{7,6},{8,9},{9,8},{10,11... | collective-permute-start | bytes 49160 | tf_op jit(solution)/shard_map/ppermute | solution.py:328
  153.7 2.3 %collective-permute-done.4 = f32[32,128]{1,0:T(8,128)S(1)} collective-permute-done((f32[32,128]{1,0:T(8,128)}, f32[32,128]{1,0:T(8,128)S(1)}, u32[]{:S(2)}, u32[]{:S(2)}) %collective-permute-start.4) | collective-permute-done | bytes 16416 | tf_op jit(solution)/shard_map/ppermute | solution.py:328
  156.0 1.3 add_bitcast_fusion
Async XLA Ops:
  6.5 58.4 %copy-start = (s32[2,128]{1,0:T(2,128)S(1)}, s32[2,128]{1,0:T(2,128)}, u32[]{:S(2)}) copy-start(s32[2,128]{1,0:T(2,128)} %param.10) | copy-start | bytes 3076
  6.5 50.6 %copy-start.6 = (s32[2]{0:T(128)S(1)}, s32[2]{0:T(128)}, u32[]{:S(2)}) copy-start(s32[2]{0:T(128)} %param.11) | copy-start | bytes 28
  6.5 106.4 %copy-start.7 = (s32[32,2]{0,1:T(2,128)S(1)}, s32[32,2]{0,1:T(2,128)}, u32[]{:S(2)}) copy-start(s32[32,2]{0,1:T(2,128)} %param.8) | copy-start | bytes 772
  10.1 46.0 %all-to-all-start = ((bf16[128,32,128]{2,1,0:T(8,128)(2,1)}), bf16[128,32,128]{2,1,0:T(8,128)(2,1)S(1)}, u32[]{:S(2)}, u32[]{:S(2)}) async-start(bf16[128,32,128]{2,1,0:T(8,128)(2,1)} %pack.1), calls=%async_computation | async-start | bytes 2097152 | tf_op jit(solution)/shard_map/all_to_all | solution.py:255
  25.0 92.7 %all-gather.2.cloned.1.call-start = ((), (), s32[]{:S(2)}) async-start(), calls=%async_computation.2 | async-start | bytes 7077888 | tf_op jit(solution)/shard_map/all_gather | solution.py:258
  26.2 29.9 %collective-permute-start.1 = (bf16[4,128,768]{2,1,0:T(8,128)(2,1)S(1)}, bf16[4,128,768]{2,1,0:T(8,128)(2,1)S(1)}, u32[]{:S(2)}, u32[]{:S(2)}) collective-permute-start(bf16[4,128,768]{2,1,0:T(8,128)(2,1)S(1)} %constant_dynamic-slice_fusion.2), channel_id=1, source_target_pairs={{0,1},{1,0},{2,3},{3,2},{4,5},{5,4},{6,7},{7,6},{8,9},{9,8},{10,11... | collective-permute-start | bytes 2359304 | tf_op jit(solution)/shard_map/ppermute | solution.py:240
  56.1 1.0 copy-start.4
  56.1 10.9 %copy-start.2 = (bf16[128,32,128]{2,1,0:T(8,128)(2,1)}, bf16[128,32,128]{2,1,0:T(8,128)(2,1)S(1)}, u32[]{:S(2)}) copy-start(bf16[128,32,128]{2,1,0:T(8,128)(2,1)S(1)} %all-to-all-done.r_ref) | copy-start | bytes 3145732
  63.0 4.0 %collective-permute-start.2 = (bf16[1,32,128]{2,1,0:T(8,128)(2,1)S(1)}, bf16[1,32,128]{2,1,0:T(8,128)(2,1)S(1)}, u32[]{:S(2)}, u32[]{:S(2)}) collective-permute-start(bf16[1,32,128]{2,1,0:T(8,128)(2,1)S(1)} %get-tuple-element.13), channel_id=1, source_target_pairs={{0,1},{1,0},{2,3},{3,2},{4,5},{5,4},{6,7},{7,6},{8,9},{9,8},{10,11... | collective-permute-start | bytes 24584 | tf_op jit(solution)/shard_map/ppermute | solution.py:261
  67.0 0.6 copy-start.5
  112.1 5.6 %copy-start.1 = (bf16[128,32,128]{2,1,0:T(8,128)(2,1)}, bf16[128,32,128]{2,1,0:T(8,128)(2,1)S(1)}, u32[]{:S(2)}) copy-start(bf16[128,32,128]{2,1,0:T(8,128)(2,1)S(1)} %all_to_all.10.far_ref.wa_ref) | copy-start | bytes 3145732
  112.1 25.3 %collective-permute-start.3 = (bf16[128,32,128]{2,1,0:T(8,128)(2,1)S(1)}, bf16[128,32,128]{2,1,0:T(8,128)(2,1)S(1)}, u32[]{:S(2)}, u32[]{:S(2)}) collective-permute-start(bf16[128,32,128]{2,1,0:T(8,128)(2,1)S(1)} %all_to_all.10.far_ref.wa_ref), channel_id=1, source_target_pairs={{0,2},{2,0},{1,3},{3,1},{4,6},{6,4},{5,7},{7,5},{8,10},{10,8},{9,1... | collective-permute-start | bytes 3145736 | tf_op jit(solution)/shard_map/ppermute | solution.py:274
  112.9 3.9 %collective-permute-start = (s32[32,2]{0,1:T(2,128)S(1)}, s32[32,2]{0,1:T(2,128)S(1)}, u32[]{:S(2)}, u32[]{:S(2)}) collective-permute-start(s32[32,2]{0,1:T(2,128)S(1)} %copy-done.7), channel_id=1, source_target_pairs={{0,1},{1,0},{2,3},{3,2},{4,5},{5,4},{6,7},{7,6},{8,9},{9,8},{10,11... | collective-permute-start | bytes 776 | tf_op jit(solution)/shard_map/ppermute | solution.py:241
  137.4 1.0 copy-start.3
  151.7 4.3 %collective-permute-start.4 = (f32[32,128]{1,0:T(8,128)}, f32[32,128]{1,0:T(8,128)S(1)}, u32[]{:S(2)}, u32[]{:S(2)}) collective-permute-start(f32[32,128]{1,0:T(8,128)} %get-tuple-element.12), channel_id=1, source_target_pairs={{0,1},{1,0},{2,3},{3,2},{4,5},{5,4},{6,7},{7,6},{8,9},{9,8},{10,11... | collective-permute-start | bytes 49160 | tf_op jit(solution)/shard_map/ppermute | solution.py:328
Sparse Core Ops, SparseCore 0:
  57.2 54.5 all-gather.1

commit v2 on v0

v2 whole, which is shorter than its diff:
```python
import functools
import math

import jax
import jax.numpy as jnp
import numpy as np
from jax import lax
from jax.experimental import pallas as pl
from jax.experimental.pallas import tpu as pltpu
from jax.sharding import Mesh
from jax.sharding import PartitionSpec as P

ATOMS = 64
ORBS = 64
AUX_ATOM = 12
BANDS = 64
OCC = 16
TRANSFERS = 2
NAUX = ATOMS * AUX_ATOM
HALF = NAUX // 2
BF = jnp.bfloat16
F32 = jnp.float32
KA = ("z", "xl", "y", "core")
BY_CORE = ("core", "z", "xl", "y")
PEERS = 128
FAR = 2 * OCC * ATOMS * ORBS // 128
FAR_ROWS = FAR // PEERS
PACKED = HALF * NAUX // 128
W_ROWS = PACKED // PEERS
PIECE = FAR_ROWS + W_ROWS
PREFACTOR = -1.0 / math.sqrt(TRANSFERS * NAUX * OCC)


def dot(a, b):
    return jnp.dot(a, b, preferred_element_type=F32)


def w_tile(row, lane):
    at = (row // 16 * (NAUX // 128) + lane // 128) * 16
    return slice(at, at + 16)


def pack_kernel(s_ref, c_ref, w_ref, triple_ref, out_ref, share_ref, stage_ref, in_sem, out_sem):
    parts = in_sem.shape[0]
    size = share_ref.shape[0] // parts
    reads, writes = [], []
    for n in range(parts):
        rows = pl.ds(n * size, size)
        reads.append(
            pltpu.make_async_copy(
                triple_ref.at[pl.ds(s_ref[1] * share_ref.shape[0] + n * size, size)],
                stage_ref.at[rows],
                in_sem.at[n],
            )
        )
        writes.append(pltpu.make_async_copy(stage_ref.at[rows], share_ref.at[rows], out_sem.at[n]))
    for copy in reads:
        copy.start()
    y = lax.broadcasted_iota(jnp.int32, (2 * OCC, 128), 0)
    col = lax.broadcasted_iota(jnp.int32, (2 * OCC, 128), 1)
    pick = (col == jnp.where(y < OCC, y, y + BANDS - OCC)).astype(F32).astype(BF)
    for ob in range(ATOMS // 2):
        far = lax.dot_general(
            pick,
            c_ref[ob * 128 : (ob + 1) * 128, :],
            (((1,), (1,)), ((), ())),
            preferred_element_type=F32,
        )
        for i in range(4):
            at = (4 * ob + i) * PIECE
            out_ref[at : at + FAR_ROWS, :] = far[i * 8 : i * 8 + 8].astype(BF)
    for read, write in zip(reads, writes):
        read.wait()
        write.start()
    row0 = s_ref[0] * HALF
    r16 = lax.broadcasted_iota(jnp.int32, (16, 128), 0)
    c16 = lax.broadcasted_iota(jnp.int32, (16, 128), 1)
    for row in range(0, HALF, 16):
        for lane in range(0, NAUX, 128):
            above = (c16 + lane) - (r16 + row) - row0
            rows = slice(row, row + 16)
            wr = w_ref[rows, lane : lane + 128].astype(F32)
            wi = w_ref[rows, NAUX + lane : NAUX + lane + 128].astype(F32)
            packed = jnp.where(above > 0, wr, jnp.where(above == 0, 0.5 * wr, wi))
            packed = packed.astype(BF)
            tile = w_tile(row, lane)
            a = tile.start
            while a < tile.stop:
                piece, at = divmod(a, W_ROWS)
                b = min(tile.stop, a - at + W_ROWS)
                to = piece * PIECE + FAR_ROWS + at
                out_ref[to : to + b - a, :] = packed[a - tile.start : b - tile.start]
                a = b
    for write in writes:
        write.wait()


def route_kernel(h_ref, partner_ref, r_ref, own_ref, got_ref, out_ref):
    split = FAR_ROWS // 2
    first = h_ref[0] == 0

    def fill(halves):
        for k in range(PEERS):
            out_ref[k, split:] = halves[k // (PEERS // 2)][0]

    pl.when(first)(lambda: fill((own_ref, got_ref)))
    pl.when(jnp.logical_not(first))(lambda: fill((got_ref, own_ref)))
    for k in range(PEERS):
        out_ref[k, 0:split] = r_ref[partner_ref[k], 0:split]


OWN_MIB = 48
GROUP = 8
GROUP_AUX = GROUP * AUX_ATOM
PITCH = GROUP_AUX + 1


def spread_far(far_ref, x_ref):
    low32 = lax.broadcasted_iota(jnp.int32, (2 * OCC, 128), 1) < ORBS
    for ob in range(ATOMS // 2):
        tops = [(4 * ob + i) * PIECE for i in range(4)]
        both = jnp.concatenate([far_ref[a : a + FAR_ROWS, :].astype(F32) for a in tops], axis=0)
        turned = pltpu.roll(both, 64, 1)
        x_ref[2 * ob] = jnp.where(low32, both, turned).astype(BF)
        x_ref[2 * ob + 1] = jnp.where(low32, turned, both).astype(BF)


def pair_kernel(s_ref, nbr_ref, far_ref, x_ref, triple_ref, coef_ref, out_ref, stage_ref, c_ref, w_ref, p_ref, sems):
    step = pl.program_id(0)
    low32 = lax.broadcasted_iota(jnp.int32, (2 * OCC, 128), 1) < ORBS

    def fetch(n):
        rows = pl.ds(n * GROUP, GROUP)
        return pltpu.make_async_copy(triple_ref.at[rows], stage_ref.at[rows], sems.at[n])

    def fetch_own():
        rows = pl.ds(pl.multiple_of(s_ref[0] * ORBS, ORBS), c_ref.shape[0])
        return pltpu.make_async_copy(coef_ref.at[rows], c_ref, sems.at[sems.shape[0] - 1])

    @pl.when(step == 0)
    def _():
        fetch(0).start()
        fetch_own().start()
        for n in range(1, stage_ref.shape[0] // GROUP):
            fetch(n).start()
        w_ref[...] = jnp.zeros_like(w_ref)
        if far_ref is not None:
            spread_far(far_ref, x_ref)
        fetch_own().wait()

    fetch(step).wait()
    for g in range(GROUP):
        at = step * GROUP + g
        n0 = nbr_ref[s_ref[1] + at, 0]
        n1 = nbr_ref[s_ref[1] + at, 1]
        lhs = jnp.where(low32, x_ref[n0].astype(F32), x_ref[n1].astype(F32)).astype(BF)
        pair = dot(lhs, stage_ref[at]).astype(BF)
        own = c_ref[pl.ds(pl.multiple_of(at * ORBS, ORBS), ORBS), :].astype(F32)
        sign = jnp.where(lax.broadcasted_iota(jnp.int32, own.shape, 1) < BANDS, 1.0, -1.0)
        first = (own * sign).astype(BF)
        second = pltpu.roll(own, BANDS, 1).astype(BF)
        w_ref[g, 0:64, 0:128] = first
        w_ref[g, 64:128, 128:256] = first
        w_ref[g, 128:192, 0:128] = second
        w_ref[g, 192:256, 128:256] = second
        left = jnp.concatenate(
            [
                jnp.concatenate(
                    [pair[0:16, q * 128 : q * 128 + 128], pair[16:32, q * 128 : q * 128 + 128]],
                    axis=1,
                )
                for q in range(AUX_ATOM // 2)
            ],
            axis=0,
        )
        prod = dot(left, w_ref[g])
        for q in range(AUX_ATOM // 2):
            for e in range(2):
                mu = g * AUX_ATOM + 2 * q + e
                for s in range(2):
                    p_ref[pl.ds(mu + s * 8 * PITCH, 8, stride=PITCH), :] = prod[
                        q * 16 + s * 8 : q * 16 + s * 8 + 8, e * 128 : e * 128 + 128
                    ]

    rows = pl.ds(pl.multiple_of(step * GROUP_AUX, GROUP_AUX), GROUP_AUX)
    for l in range(OCC):
        out_ref[l, rows, :] = p_ref[l * PITCH : l * PITCH + GROUP_AUX, :].astype(BF)


def pair_products(first, row, nbr, x, triple, coef, into=None, mib=24):
    count = triple.shape[0]
    extra = () if into is None else (into,)

    def kernel(s_ref, nbr_ref, x_ref, triple_ref, c_ref, *rest):
        if extra:
            pair_kernel(s_ref, nbr_ref, None, x_ref, triple_ref, c_ref, *rest[len(extra) :])
        else:
            out_ref, made_ref, *scratch = rest
            pair_kernel(s_ref, nbr_ref, x_ref, made_ref, triple_ref, c_ref, out_ref, *scratch)

    vmem = pl.BlockSpec(memory_space=pltpu.VMEM)
    out_shape = jax.ShapeDtypeStruct((OCC, NAUX, 128), BF)
    out_spec = pl.BlockSpec((OCC, count * AUX_ATOM, 128), lambda i, s, _: (0, s[0] // count, 0))
    made = jax.ShapeDtypeStruct((ATOMS, 2 * OCC, 128), BF)
    return pl.pallas_call(
        kernel,
        out_shape=out_shape if extra else (out_shape, made),
        grid_spec=pltpu.PrefetchScalarGridSpec(
            num_scalar_prefetch=2,
            grid=(count // GROUP,),
            in_specs=[
                whole(made.shape) if extra else vmem,
                pl.BlockSpec(memory_space=pltpu.HBM),
                pl.BlockSpec(memory_space=pltpu.HBM),
                *(pl.BlockSpec(memory_space=pl.ANY) for _ in extra),
            ],
            out_specs=out_spec if extra else (out_spec, whole(made.shape)),
            scratch_shapes=[
                pltpu.VMEM(triple.shape, BF),
                pltpu.VMEM((count * ORBS, 128), BF),
                pltpu.VMEM((GROUP, 256, 256), BF),
                pltpu.VMEM((OCC * PITCH + 8, 128), F32),
                pltpu.SemaphoreType.DMA((count // GROUP + 1,)),
            ],
        ),
        input_output_aliases={5: 0} if extra else {},
        compiler_params=params(mib),
        cost_estimate=pl.CostEstimate(
            flops=count * 200_000_000, bytes_accessed=count * 250_000, transcendentals=0
        ),
        name="pair_products",
    )(jnp.stack([first, row]), nbr, x, triple, coef, *extra)


BLK = 256
NB = NAUX // BLK
BATCH = 4


def sigma_kernel(s_ref, p_ref, wa_ref, wb_ref, keep_ref, send_ref, re_ref, im_ref, acc_ref, sig_ref):
    step = pl.program_id(0)

    @pl.when(step == 0)
    def _():
        core0 = s_ref[1] == 0
        r16 = lax.broadcasted_iota(jnp.int32, (16, 128), 0)
        c16 = lax.broadcasted_iota(jnp.int32, (16, 128), 1)
        for half in range(2):
            for row in range(0, HALF, 16):
                for lane in range(0, NAUX, 128):
                    here = wa_ref[w_tile(row, lane), :].astype(F32)
                    there = wb_ref[w_tile(row, lane), :].astype(F32)
                    tile = jnp.where(core0, there, here) if half else jnp.where(core0, here, there)
                    mu = half * HALF + row
                    above = (c16 + lane) - (r16 + mu)
                    at = (slice(mu, mu + 16), slice(lane, lane + 128))
                    if lane // BLK >= mu // BLK:
                        re_ref[at] = jnp.where(above >= 0, tile, 0.0).astype(BF)
                    if lane // BLK <= mu // BLK:
                        im_ref[at] = jnp.where(above < 0, tile, 0.0).astype(BF)
        acc_ref[...] = jnp.zeros_like(acc_ref)

    p = [p_ref[s] for s in range(BATCH)]
    wide = jnp.concatenate(p, axis=1)
    acc = acc_ref[...]
    for blk in range(NB):
        a, b = blk * BLK, blk * BLK + BLK
        re = dot(re_ref[a:b, a:NAUX], wide[a:NAUX]).astype(BF)
        im = dot(im_ref[a:b, 0:b], wide[0:b]).astype(BF)
        for s in range(BATCH):
            lanes = slice(s * 128, s * 128 + 128)
            acc += lax.dot_general(
                p[s][a:b],
                jnp.concatenate([re[:, lanes], im[:, lanes]], axis=1),
                (((0,), (0,)), ((), ())),
                preferred_element_type=F32,
            )
    acc_ref[...] = acc

    @pl.when(step == pl.num_programs(0) - 1)
    def _():
        yi = acc_ref[:, 128:256]
        low = lax.broadcasted_iota(jnp.int32, yi.shape, 1) < BANDS
        turned = pltpu.roll(yi, BANDS, 1)
        y = acc_ref[:, 0:128] + jnp.where(low, -turned, turned)
        z = y + y.T
        re = z[:BANDS, :BANDS] + z[BANDS:, BANDS:]
        im = z[:BANDS, BANDS:] - z[BANDS:, :BANDS]
        sig_ref[...] = PREFACTOR * jnp.concatenate([re, im], axis=1)
        h = s_ref[0]
        rows = BANDS // 2
        keep_ref[...] = sig_ref[pl.ds(pl.multiple_of(h * rows, rows), rows), :]
        send_ref[...] = sig_ref[pl.ds(pl.multiple_of((1 - h) * rows, rows), rows), :]


def screened_sigma(h, core, products, here, there):
    rows = BANDS // 2
    part = jax.ShapeDtypeStruct((rows, 2 * BANDS), F32)
    return pl.pallas_call(
        sigma_kernel,
        out_shape=(part, part),
        grid=(OCC // BATCH,),
        in_specs=[
            pl.BlockSpec(memory_space=pltpu.SMEM),
            pl.BlockSpec((BATCH, NAUX, 128), lambda i: (i, 0, 0)),
            pl.BlockSpec(memory_space=pltpu.VMEM),
            pl.BlockSpec(memory_space=pltpu.VMEM),
        ],
        out_specs=(whole((rows, 2 * BANDS)),) * 2,
        scratch_shapes=[
            pltpu.VMEM((NAUX, NAUX), BF),
            pltpu.VMEM((NAUX, NAUX), BF),
            pltpu.VMEM((128, 256), F32),
            pltpu.VMEM((BANDS, 128), F32),
        ],
        compiler_params=params(24),
        name="screened_sigma",
    )(jnp.stack([h, core]), products, here, there)


def place(k):
    return k % 2 * (PEERS // 2) + k // 2


def by_core(ids):
    return place(ids).reshape(PEERS // 2, 2).T.reshape(PEERS)


def params(mib):
    return pltpu.CompilerParams(vmem_limit_bytes=mib * 2**20)


def whole(shape):
    return pl.BlockSpec(shape, lambda i, *_: (0,) * len(shape))


def x_crossing():
    ids = np.arange(8 * 2 * 4 * 2 * 2).reshape(8, 2, 4, 2, 2)
    pairs = []
    for z, xl, y, core, aux in np.ndindex(ids.shape):
        pairs.append((int(ids[z, xl, y, core, aux]), int(ids[z, 1 - xl, y, core, 1 - aux])))
    return pairs


def local(coefficients, triple, neighbors, w_screened, partner, q_ids):
    h = lax.axis_index("aux").astype(jnp.int32)
    me = lax.axis_index(KA).astype(jnp.int32)
    core = lax.axis_index("core").astype(jnp.int32)
    swap = [(0, 1), (1, 0)]
    atoms = triple.shape[0]
    coef = coefficients[0]
    triple = triple.reshape(atoms, 2 * ORBS, AUX_ATOM * ORBS)

    share = atoms // 2
    nbr_other = lax.ppermute(neighbors, "aux", swap)

    smem = pl.BlockSpec(memory_space=pltpu.SMEM)
    vmem = pl.BlockSpec(memory_space=pltpu.VMEM)
    hbm = pl.BlockSpec(memory_space=pl.ANY)
    shared = (share, *triple.shape[1:])
    pieces, sent = pl.pallas_call(
        pack_kernel,
        out_shape=(
            jax.ShapeDtypeStruct((PEERS * PIECE, 128), BF),
            jax.ShapeDtypeStruct(shared, BF),
        ),
        in_specs=[smem, vmem, vmem, hbm],
        out_specs=(vmem, hbm),
        scratch_shapes=[
            pltpu.VMEM(shared, BF),
            pltpu.SemaphoreType.DMA((4,)),
            pltpu.SemaphoreType.DMA((4,)),
        ],
        compiler_params=params(56),
        name="pack",
    )(jnp.stack([h, core]), coef, w_screened[0], triple)
    crossed = lax.ppermute(sent, (*KA, "aux"), x_crossing())

    spread = lax.all_to_all(
        pieces.reshape(PEERS, PIECE // 2, 2, 128), BY_CORE, split_axis=0, concat_axis=0, tiled=True
    )
    partner_here = by_core(lax.dynamic_slice_in_dim(partner, h, 1, 0)[0])
    partner_here, q_place, nbr_other = lax.optimization_barrier(
        (partner_here, place(q_ids), nbr_other)
    )
    split = FAR_ROWS // 2

    def own_piece(t):
        return lax.dynamic_slice(spread, (q_place[t], split, 0, 0), (1, W_ROWS // 2, 2, 128))

    got = lax.ppermute(own_piece(1 - h), "aux", swap)
    routed = pl.pallas_call(
        route_kernel,
        out_shape=jax.ShapeDtypeStruct(spread.shape, BF),
        in_specs=[smem, smem, vmem, vmem, vmem],
        out_specs=vmem,
        compiler_params=params(12),
        name="route",
    )(h[None], partner_here, spread, own_piece(h), got)
    arrived = lax.all_to_all(routed, BY_CORE, split_axis=0, concat_axis=0, tiled=True)

    crossed, arrived = lax.optimization_barrier((crossed, arrived))
    crossed2 = lax.ppermute(crossed, "core", swap)
    here = arrived[:, split:].reshape(PACKED, 128)
    there = lax.ppermute(here, "core", swap)
    far = arrived.reshape(PEERS * PIECE, 128)
    zero = jnp.zeros_like(h)
    others = (1 - h) * atoms
    products, x = pair_products(h * atoms, zero, neighbors, far, triple, coef, mib=OWN_MIB)
    near, away = core * share, (1 - core) * share
    products = pair_products(others + near, near, nbr_other, x, crossed, coef, products)
    products = pair_products(others + away, away, nbr_other, x, crossed2, coef, products)
    keep, send = screened_sigma(h, core, products, here, there)
    return (keep + lax.ppermute(send, "aux", swap))[None]


def solution(mesh):
    ka, aux = mesh.devices.shape
    fine = Mesh(mesh.devices.reshape(8, 2, 4, 2, aux), (*KA, "aux"))
    in_specs = (
        P(KA, None, None),
        P("aux", None, None, None),
        P("aux", None),
        P(KA, "aux", None),
        P(),
        P(),
    )
    return jax.shard_map(
        local, mesh=fine, in_specs=in_specs, out_specs=P(KA, "aux", None), check_vma=False
    )
```

time: 1270 us -> 125 us (0.10)
  waiting for transfers between devices: 1090 us -> 54.2 us
  other arithmetic: 58.1 us -> 1.45 us
  local copies, waits for them, and re-layouts: 46 us -> 1.48 us
  Pallas kernels: 0 us -> 32.1 us
  matrix products: 28.7 us -> 0 us
  between operations: 16.7 us -> 3.87 us
    psum x1 -> x0, waiting for transfers between devices: 963 us -> none  [from_root(): return lax.psum(block, axis)]
    all_gather x1 -> x0, waiting for transfers between devices: 70.2 us -> none  [local(): gathered = lax.all_gather(products, 'aux', axis=2, tiled=True)]
    ppermute x0 -> x6, waiting for transfers between devices: none -> 39.8 us  [the longest x1 31.8 us: local(): crossed = lax.ppermute(sent, (*KA, 'aux'), x_crossing())]
    concatenate x3 -> x0, other arithmetic: 37.8 us -> none  [the longest x1 34.4 us: local(): jnp.concatenate([gathered, rotated_parts(gathered, band_count)], axis=2)]
    pallas_call x0 -> x6, Pallas kernels: none -> 32.1 us  [the longest x3 17.1 us: pair_products(): pl.pallas_call(kernel, out_shape=out_shape if extra else (out_shape, made...]
    dot_general x5 -> x0, matrix products: 28.7 us -> none  [the longest x2 15.4 us: local(): jnp.einsum('ab,kbx->kax', screens[momentum_transfer], stacked[momentum_tr...]
    all_to_all x3 -> x2, waiting for transfers between devices: 41.4 us -> 14.4 us  [the longest x1 14.4 us: local(): lax.all_to_all(pieces.reshape(PEERS, PIECE // 2, 2, 128), BY_CORE, split_...]
    reduce_scatter x1 -> x0, waiting for transfers between devices: 15.6 us -> none  [local(): lax.psum_scatter(local_sigma.astype(jnp.bfloat16), 'aux', scatter_dimensi...]
  transfers between devices with their start and end apart: 6 -> 8, of which waited for: 6 -> 5; matrix products, arithmetic and copies ran while one was open for 5% -> 1% of each run, Pallas kernels for 0% -> 15%
where the time goes in v2:
time: 125 us
  waiting for transfers between devices  54.2 us (43%)
  Pallas kernels  32.1 us (26%)
  starting transfers between devices  31.4 us (25%)
  between operations  3.87 us (3%)
  local copies, waits for them, and re-layouts  1.48 us (1%)
  other arithmetic  1.45 us (1%)
    ppermute x1, waiting for transfers between devices, local(): crossed = lax.ppermute(sent, (*KA, 'aux'), x_crossing())  31.8 us
    pallas_call x3, Pallas kernels, pair_products(): pl.pallas_call(kernel, out_shape=out_shape if extra else (out_shape, made...  17.1 us
    all_to_all x1, starting transfers between devices, local(): lax.all_to_all(pieces.reshape(PEERS, PIECE // 2, 2, 128), BY_CORE, split_...  15.3 us
    all_to_all x1, waiting for transfers between devices, local(): lax.all_to_all(pieces.reshape(PEERS, PIECE // 2, 2, 128), BY_CORE, split_...  14.4 us
    pallas_call x1, Pallas kernels, screened_sigma(): pl.pallas_call(sigma_kernel, out_shape=(part, part), grid=(OCC // BATCH,)...  7.7 us
    all_to_all x1, starting transfers between devices, local(): lax.all_to_all(routed, BY_CORE, split_axis=0, concat_axis=0, tiled=True)  7.24 us
    pallas_call x1, Pallas kernels, local(): pl.pallas_call(pack_kernel, out_shape=(jax.ShapeDtypeStruct((PEERS * PIEC...  5.42 us
    ppermute x1, waiting for transfers between devices, local(): nbr_other = lax.ppermute(neighbors, 'aux', swap)  3.5 us
  transfers between devices with their start and end apart: 8, of which 5 were waited for; matrix products, arithmetic and copies ran while one was open for 1% of the time, Pallas kernels for 15%

profile of v2, /device:TPU:1, one launch (start us, length us, event | category | flops | bytes accessed | tf_op | source)
XLA Modules:
  0.0 124.6 jit_solution(13416906103760177781)
XLA Ops:
  0.0 0.0 copy-start
  0.0 0.6 pad_add_fusion
  0.6 0.0 copy-start.3
  0.6 0.0 copy-start.4
  0.6 5.4 %pack.1 = (bf16[3328,128]{1,0:T(8,128)(2,1)}, bf16[16,128,768]{2,1,0:T(8,128)(2,1)}) custom-call(s32[2]{0:T(128)} %get-tuple-element.31.s_ref, bf16[4096,128]{1,0:T(8,128)(2,1)} %bitcast.22, bf16[384,1536]{1,0:T(8,128)(2,1)} %bitcast.28, bf16[32,128,768]{2,1,0:T(8,128)(2,1)} %bitcast.26), custom_call_target="tpu_custom_call" | custom-call | tf_op jit(solution)/shard_map/pack/pallas_call | solution.py:361
  6.1 0.0 copy-start.1
  6.1 15.3 %all-to-all-start = ((bf16[128,13,2,128]{3,2,1,0:T(2,128)(2,1)}), bf16[128,13,2,128]{3,2,1,0:T(2,128)(2,1)S(1)}, u32[]{:S(2)}, u32[]{:S(2)}) async-start(bf16[128,13,2,128]{3,2,1,0:T(2,128)(2,1)} %bitcast.29), calls=%async_computation | async-start | bytes 1703936 | tf_op jit(solution)/shard_map/all_to_all | solution.py:379
  21.4 2.7 %collective-permute-start.1 = (bf16[16,128,768]{2,1,0:T(8,128)(2,1)}, bf16[16,128,768]{2,1,0:T(8,128)(2,1)}, u32[]{:S(2)}, u32[]{:S(2)}) collective-permute-start(bf16[16,128,768]{2,1,0:T(8,128)(2,1)} %get-tuple-element.17), channel_id=1, source_target_pairs={{0,17},{1,16},{2,19},{3,18},{4,21},{5,20},{6,23},{7,22},{8,25},{9,... | collective-permute-start | bytes 9437192 | tf_op jit(solution)/shard_map/ppermute | solution.py:377
  24.2 0.0 copy-done.3
  24.2 0.1 copy.13.nbr_ref
  24.2 0.5 collective-permute-start
  24.8 0.0 copy-done
  24.8 0.1 squeeze.15
  25.0 0.1 copy.12
  25.1 0.1 reshape.17.partner_ref
  25.1 0.0 copy-done.4
  25.2 3.5 %collective-permute-done.nbr_ref = s32[32,2]{1,0:T(8,128)S(1)} collective-permute-done((s32[32,2]{1,0:T(8,128)S(1)}, s32[32,2]{1,0:T(8,128)S(1)}, u32[]{:S(2)}, u32[]{:S(2)}) %collective-permute-start) | collective-permute-done | bytes 288 | tf_op jit(solution)/shard_map/ppermute | solution.py:355
  28.7 0.7 fusion.10
  33.0 14.4 %all-to-all-done.r_ref = bf16[128,13,2,128]{3,2,1,0:T(2,128)(2,1)S(1)} async-done(((bf16[128,13,2,128]{3,2,1,0:T(2,128)(2,1)}), bf16[128,13,2,128]{3,2,1,0:T(2,128)(2,1)S(1)}, u32[]{:S(2)}, u32[]{:S(2)}) %all-to-all-start) | async-done | bytes 852000 | tf_op jit(solution)/shard_map/all_to_all | solution.py:379
  47.5 2.5 %collective-permute-start.2 = (bf16[1,9,2,128]{3,2,1,0:T(2,128)(2,1)S(1)}, bf16[1,9,2,128]{3,2,1,0:T(2,128)(2,1)S(1)}, u32[]{:S(2)}, u32[]{:S(2)}) collective-permute-start(bf16[1,9,2,128]{3,2,1,0:T(2,128)(2,1)S(1)} %get-tuple-element.27), channel_id=1, source_target_pairs={{0,1},{1,0},{2,3},{3,2},{4,5},{5,4},{6,7},{7,6},{8,9},{9,8},{10,11... | collective-permute-start | bytes 13832 | tf_op jit(solution)/shard_map/ppermute | solution.py:391
  50.0 1.6 %collective-permute-done.2.got_ref = bf16[1,9,2,128]{3,2,1,0:T(2,128)(2,1)S(1)} collective-permute-done((bf16[1,9,2,128]{3,2,1,0:T(2,128)(2,1)S(1)}, bf16[1,9,2,128]{3,2,1,0:T(2,128)(2,1)S(1)}, u32[]{:S(2)}, u32[]{:S(2)}) %collective-permute-start.2) | collective-permute-done | bytes 4640 | tf_op jit(solution)/shard_map/ppermute | solution.py:391
  51.6 1.9 %route.1 = bf16[128,13,2,128]{3,2,1,0:T(2,128)(2,1)} custom-call(s32[1]{0:T(128)} %bitcast.h_ref, s32[128]{0:T(128)S(1)} %reshape.17.partner_ref, bf16[128,13,2,128]{3,2,1,0:T(2,128)(2,1)S(1)} %all-to-all-done.r_ref, bf16[1,9,2,128]{3,2,1,0:T(2,128)(2,1)S(1)} %get-tuple-element.28.own_ref, bf16[1,9,2,128]{3,2,1,0:T(2,128)(2,1)S(1)} %collective-permute-done.2.got_ref), custom_call_target="tpu_custom_call" | custom-call | tf_op jit(solution)/shard_map/route/pallas_call | solution.py:392
  53.5 7.2 %all-to-all-start.1 = ((bf16[128,13,2,128]{3,2,1,0:T(2,128)(2,1)}), bf16[128,13,2,128]{3,2,1,0:T(2,128)(2,1)S(1)}, u32[]{:S(2)}, u32[]{:S(2)}) async-start(bf16[128,13,2,128]{3,2,1,0:T(2,128)(2,1)} %route.1), calls=%async_computation.1 | async-start | bytes 1703936 | tf_op jit(solution)/shard_map/all_to_all | solution.py:400
  60.8 31.8 %collective-permute-done.1.triple_ref = bf16[16,128,768]{2,1,0:T(8,128)(2,1)} collective-permute-done((bf16[16,128,768]{2,1,0:T(8,128)(2,1)}, bf16[16,128,768]{2,1,0:T(8,128)(2,1)}, u32[]{:S(2)}, u32[]{:S(2)}) %collective-permute-start.1) | collective-permute-done | bytes 3145760 | tf_op jit(solution)/shard_map/ppermute | solution.py:377
  92.6 0.0 all-to-all-done.1
  92.6 1.4 %collective-permute-start.3 = (bf16[16,128,768]{2,1,0:T(8,128)(2,1)}, bf16[16,128,768]{2,1,0:T(8,128)(2,1)}, u32[]{:S(2)}, u32[]{:S(2)}) collective-permute-start(bf16[16,128,768]{2,1,0:T(8,128)(2,1)} %collective-permute-done.1.triple_ref), channel_id=1, source_target_pairs={{0,2},{2,0},{1,3},{3,1},{4,6},{6,4},{5,7},{7,5},{8,10},{10,8},{9,1... | collective-permute-start | bytes 9437192 | tf_op jit(solution)/shard_map/ppermute | solution.py:403
  94.0 0.1 pad_add_fusion.3.s_ref
  94.1 0.1 pad_add_fusion.1.s_ref
  94.2 0.4 slice.3
  94.6 0.3 collective-permute-start.4
  94.8 0.0 copy-done.1
  94.9 7.4 %pair_products.3 = (bf16[16,768,128]{2,1,0:T(8,128)(2,1)S(1)}, bf16[64,32,128]{2,1,0:T(8,128)(2,1)S(1)}) custom-call(s32[2]{0:T(128)S(1)} %get-tuple-element.32.s_ref, s32[32,2]{1,0:T(8,128)S(1)} %copy.13.nbr_ref, bf16[3328,128]{1,0:T(8,128)(2,1)S(1)} %bitcast.19, bf16[32,128,768]{2,1,0:T(8,128)(2,1)} %bitcast.27, bf16[4096,128]{1,0:T(8,128)(2,1)S(1)} %bitcast.23), custom_call_target="tpu_custom_call" | custom-call | flops 6400000000 | bytes 8000000 | tf_op jit(solution)/shard_map/pair_products/pallas_call | solution.py:205
  102.3 4.8 %pair_products.4.rest_0_ = bf16[16,768,128]{2,1,0:T(8,128)(2,1)S(1)} custom-call(s32[2]{0:T(128)S(1)} %pad_add_fusion.3.s_ref, s32[32,2]{1,0:T(8,128)S(1)} %collective-permute-done.nbr_ref, bf16[64,32,128]{2,1,0:T(8,128)(2,1)S(1)} %get-tuple-element.22.x_ref, ...), custom_call_target="tpu_custom_call", output_to_operand_aliasing={{}: (5, {})} | custom-call | flops 3200000000 | bytes 4000000 | tf_op jit(solution)/shard_map/pair_products/pallas_call | solution.py:205
  107.2 0.0 copy-start.2
  107.2 0.0 collective-permute-done.3.triple_ref
  107.2 4.8 %pair_products.5.p_ref = bf16[16,768,128]{2,1,0:T(8,128)(2,1)S(1)} custom-call(s32[2]{0:T(128)S(1)} %pad_add_fusion.1.s_ref, s32[32,2]{1,0:T(8,128)S(1)} %collective-permute-done.nbr_ref, bf16[64,32,128]{2,1,0:T(8,128)(2,1)S(1)} %get-tuple-element.22.x_ref, bf16[16,128,768]{2,1,0:T(8,128)(2,1)} %collective-permute-done.3.triple_ref, ...), custom_call_target="tpu_custom_call", output_to_operand_aliasing={{}: (5, {})} | custom-call | flops 3200000000 | bytes 4000000 | tf_op jit(solution)/shard_map/pair_products/pallas_call | solution.py:205
  112.0 0.0 collective-permute-done.4.wb_ref
  112.0 0.0 copy-done.2
  112.1 7.7 %screened_sigma.1 = (f32[32,128]{1,0:T(8,128)S(1)}, f32[32,128]{1,0:T(8,128)S(1)}) custom-call(s32[2]{0:T(128)S(1)} %copy-done.2, bf16[16,768,128]{2,1,0:T(8,128)(2,1)S(1)} %pair_products.5.p_ref, bf16[2304,128]{1,0:T(8,128)(2,1)S(1)} %bitcast.21, bf16[2304,128]{1,0:T(8,128)(2,1)S(1)} %collective-permute-done.4.wb_ref), custom_call_target="tpu_custom_call" | custom-call | tf_op jit(solution)/shard_map/screened_sigma/pallas_call | solution.py:299
  119.8 1.3 %collective-permute-start.5 = (f32[32,128]{1,0:T(8,128)S(1)}, f32[32,128]{1,0:T(8,128)S(1)}, u32[]{:S(2)}, u32[]{:S(2)}) collective-permute-start(f32[32,128]{1,0:T(8,128)S(1)} %get-tuple-element.26), channel_id=1, source_target_pairs={{0,1},{1,0},{2,3},{3,2},{4,5},{5,4},{6,7},{7,6},{8,9},{9,8},{10,11... | collective-permute-start | bytes 49160 | tf_op jit(solution)/shard_map/ppermute | solution.py:414
  121.1 2.9 %collective-permute-done.5 = f32[32,128]{1,0:T(8,128)S(1)} collective-permute-done((f32[32,128]{1,0:T(8,128)S(1)}, f32[32,128]{1,0:T(8,128)S(1)}, u32[]{:S(2)}, u32[]{:S(2)}) %collective-permute-start.5) | collective-permute-done | bytes 16416 | tf_op jit(solution)/shard_map/ppermute | solution.py:414
  123.9 0.6 add_bitcast_fusion
  (4 shorter events, 0.1 us)
Async XLA Ops:
  0.0 24.8 %copy-start = (s32[2,128]{1,0:T(2,128)S(1)}, s32[2,128]{1,0:T(2,128)}, u32[]{:S(2)}) copy-start(s32[2,128]{1,0:T(2,128)} %param.10) | copy-start | bytes 3076
  0.6 23.5 %copy-start.3 = (s32[32,2]{0,1:T(2,128)S(1)}, s32[32,2]{0,1:T(2,128)}, u32[]{:S(2)}) copy-start(s32[32,2]{0,1:T(2,128)} %param.8) | copy-start | bytes 772
  0.6 24.5 %copy-start.4 = (s32[2]{0:T(128)S(1)}, s32[2]{0:T(128)}, u32[]{:S(2)}) copy-start(s32[2]{0:T(128)} %param.11) | copy-start | bytes 28
  6.1 88.8 %copy-start.1 = (bf16[1,4096,128]{2,1,0:T(8,128)(2,1)S(1)}, bf16[1,4096,128]{2,1,0:T(8,128)(2,1)}, u32[]{:S(2)}) copy-start(bf16[1,4096,128]{2,1,0:T(8,128)(2,1)} %param.6) | copy-start | bytes 3145732
  6.1 41.4 %all-to-all-start = ((bf16[128,13,2,128]{3,2,1,0:T(2,128)(2,1)}), bf16[128,13,2,128]{3,2,1,0:T(2,128)(2,1)S(1)}, u32[]{:S(2)}, u32[]{:S(2)}) async-start(bf16[128,13,2,128]{3,2,1,0:T(2,128)(2,1)} %bitcast.29), calls=%async_computation | async-start | bytes 1703936 | tf_op jit(solution)/shard_map/all_to_all | solution.py:379
  21.4 71.1 %collective-permute-start.1 = (bf16[16,128,768]{2,1,0:T(8,128)(2,1)}, bf16[16,128,768]{2,1,0:T(8,128)(2,1)}, u32[]{:S(2)}, u32[]{:S(2)}) collective-permute-start(bf16[16,128,768]{2,1,0:T(8,128)(2,1)} %get-tuple-element.17), channel_id=1, source_target_pairs={{0,17},{1,16},{2,19},{3,18},{4,21},{5,20},{6,23},{7,22},{8,25},{9,... | collective-permute-start | bytes 9437192 | tf_op jit(solution)/shard_map/ppermute | solution.py:377
  24.2 4.4 %collective-permute-start = (s32[32,2]{1,0:T(8,128)S(1)}, s32[32,2]{1,0:T(8,128)S(1)}, u32[]{:S(2)}, u32[]{:S(2)}) collective-permute-start(s32[32,2]{1,0:T(8,128)S(1)} %copy.13.nbr_ref), channel_id=1, source_target_pairs={{0,1},{1,0},{2,3},{3,2},{4,5},{5,4},{6,7},{7,6},{8,9},{9,8},{10,11... | collective-permute-start | bytes 776 | tf_op jit(solution)/shard_map/ppermute | solution.py:355
  47.5 4.2 %collective-permute-start.2 = (bf16[1,9,2,128]{3,2,1,0:T(2,128)(2,1)S(1)}, bf16[1,9,2,128]{3,2,1,0:T(2,128)(2,1)S(1)}, u32[]{:S(2)}, u32[]{:S(2)}) collective-permute-start(bf16[1,9,2,128]{3,2,1,0:T(2,128)(2,1)S(1)} %get-tuple-element.27), channel_id=1, source_target_pairs={{0,1},{1,0},{2,3},{3,2},{4,5},{5,4},{6,7},{7,6},{8,9},{9,8},{10,11... | collective-permute-start | bytes 13832 | tf_op jit(solution)/shard_map/ppermute | solution.py:391
  53.5 39.1 %all-to-all-start.1 = ((bf16[128,13,2,128]{3,2,1,0:T(2,128)(2,1)}), bf16[128,13,2,128]{3,2,1,0:T(2,128)(2,1)S(1)}, u32[]{:S(2)}, u32[]{:S(2)}) async-start(bf16[128,13,2,128]{3,2,1,0:T(2,128)(2,1)} %route.1), calls=%async_computation.1 | async-start | bytes 1703936 | tf_op jit(solution)/shard_map/all_to_all | solution.py:400
  92.6 14.6 %collective-permute-start.3 = (bf16[16,128,768]{2,1,0:T(8,128)(2,1)}, bf16[16,128,768]{2,1,0:T(8,128)(2,1)}, u32[]{:S(2)}, u32[]{:S(2)}) collective-permute-start(bf16[16,128,768]{2,1,0:T(8,128)(2,1)} %collective-permute-done.1.triple_ref), channel_id=1, source_target_pairs={{0,2},{2,0},{1,3},{3,1},{4,6},{6,4},{5,7},{7,5},{8,10},{10,8},{9,1... | collective-permute-start | bytes 9437192 | tf_op jit(solution)/shard_map/ppermute | solution.py:403
  94.6 17.5 %collective-permute-start.4 = (bf16[2304,128]{1,0:T(8,128)(2,1)S(1)}, bf16[2304,128]{1,0:T(8,128)(2,1)S(1)}, u32[]{:S(2)}, u32[]{:S(2)}) collective-permute-start(bf16[2304,128]{1,0:T(8,128)(2,1)S(1)} %bitcast.20), channel_id=1, source_target_pairs={{0,2},{2,0},{1,3},{3,1},{4,6},{6,4},{5,7},{7,5},{8,10},{10,8},{9,1... | collective-permute-start | bytes 1769480 | tf_op jit(solution)/shard_map/ppermute | solution.py:405
  107.2 4.9 %copy-start.2 = (s32[2]{0:T(128)S(1)}, s32[2]{0:T(128)}, u32[]{:S(2)}) copy-start(s32[2]{0:T(128)} %get-tuple-element.31.s_ref) | copy-start | bytes 28
  119.8 4.2 %collective-permute-start.5 = (f32[32,128]{1,0:T(8,128)S(1)}, f32[32,128]{1,0:T(8,128)S(1)}, u32[]{:S(2)}, u32[]{:S(2)}) collective-permute-start(f32[32,128]{1,0:T(8,128)S(1)} %get-tuple-element.26), channel_id=1, source_target_pairs={{0,1},{1,0},{2,3},{3,2},{4,5},{5,4},{6,7},{7,6},{8,9},{9,8},{10,11... | collective-permute-start | bytes 49160 | tf_op jit(solution)/shard_map/ppermute | solution.py:414

commit v3 on v2

--- a/solution.py
+++ b/solution.py
@@ -40,22 +40,7 @@
     return slice(at, at + 16)
 
 
-def pack_kernel(s_ref, c_ref, w_ref, triple_ref, out_ref, share_ref, stage_ref, in_sem, out_sem):
-    parts = in_sem.shape[0]
-    size = share_ref.shape[0] // parts
-    reads, writes = [], []
-    for n in range(parts):
-        rows = pl.ds(n * size, size)
-        reads.append(
-            pltpu.make_async_copy(
-                triple_ref.at[pl.ds(s_ref[1] * share_ref.shape[0] + n * size, size)],
-                stage_ref.at[rows],
-                in_sem.at[n],
-            )
-        )
-        writes.append(pltpu.make_async_copy(stage_ref.at[rows], share_ref.at[rows], out_sem.at[n]))
-    for copy in reads:
-        copy.start()
+def pack_kernel(h_ref, c_ref, w_ref, out_ref):
     y = lax.broadcasted_iota(jnp.int32, (2 * OCC, 128), 0)
     col = lax.broadcasted_iota(jnp.int32, (2 * OCC, 128), 1)
     pick = (col == jnp.where(y < OCC, y, y + BANDS - OCC)).astype(F32).astype(BF)
@@ -69,10 +54,7 @@
         for i in range(4):
             at = (4 * ob + i) * PIECE
             out_ref[at : at + FAR_ROWS, :] = far[i * 8 : i * 8 + 8].astype(BF)
-    for read, write in zip(reads, writes):
-        read.wait()
-        write.start()
-    row0 = s_ref[0] * HALF
+    row0 = h_ref[0] * HALF
     r16 = lax.broadcasted_iota(jnp.int32, (16, 128), 0)
     c16 = lax.broadcasted_iota(jnp.int32, (16, 128), 1)
     for row in range(0, HALF, 16):
@@ -91,8 +73,6 @@
                 to = piece * PIECE + FAR_ROWS + at
                 out_ref[to : to + b - a, :] = packed[a - tile.start : b - tile.start]
                 a = b
-    for write in writes:
-        write.wait()
 
 
 def route_kernel(h_ref, partner_ref, r_ref, own_ref, got_ref, out_ref):
@@ -118,20 +98,24 @@
 def spread_far(far_ref, x_ref):
     low32 = lax.broadcasted_iota(jnp.int32, (2 * OCC, 128), 1) < ORBS
     for ob in range(ATOMS // 2):
-        tops = [(4 * ob + i) * PIECE for i in range(4)]
+        tops = [(4 * ob + i) * FAR_ROWS for i in range(4)]
         both = jnp.concatenate([far_ref[a : a + FAR_ROWS, :].astype(F32) for a in tops], axis=0)
         turned = pltpu.roll(both, 64, 1)
         x_ref[2 * ob] = jnp.where(low32, both, turned).astype(BF)
         x_ref[2 * ob + 1] = jnp.where(low32, turned, both).astype(BF)
 
 
-def pair_kernel(s_ref, nbr_ref, far_ref, x_ref, triple_ref, coef_ref, out_ref, stage_ref, c_ref, w_ref, p_ref, sems):
+def pair_kernel(s_ref, nbr_ref, far_ref, x_ref, triple_refs, coef_ref, out_ref, stage_ref, c_ref, w_ref, p_ref, sems):
     step = pl.program_id(0)
     low32 = lax.broadcasted_iota(jnp.int32, (2 * OCC, 128), 1) < ORBS
 
+    count = stage_ref.shape[0]
+    steps = count // GROUP
+    each = steps // len(triple_refs)
+
     def fetch(n):
-        rows = pl.ds(n * GROUP, GROUP)
-        return pltpu.make_async_copy(triple_ref.at[rows], stage_ref.at[rows], sems.at[n])
+        source = triple_refs[n // each].at[pl.ds(n % each * GROUP, GROUP)]
+        return pltpu.make_async_copy(source, stage_ref.at[pl.ds(n * GROUP, GROUP)], sems.at[n])
 
     def fetch_own():
         rows = pl.ds(pl.multiple_of(s_ref[0] * ORBS, ORBS), c_ref.shape[0])
@@ -141,20 +125,22 @@
     def _():
         fetch(0).start()
         fetch_own().start()
-        for n in range(1, stage_ref.shape[0] // GROUP):
+        for n in range(1, steps):
             fetch(n).start()
         w_ref[...] = jnp.zeros_like(w_ref)
         if far_ref is not None:
             spread_far(far_ref, x_ref)
         fetch_own().wait()
 
-    fetch(step).wait()
+    for n in range(steps):
+        pl.when(step == n)(fetch(n).wait)
+    first_at = step * GROUP
     for g in range(GROUP):
-        at = step * GROUP + g
-        n0 = nbr_ref[s_ref[1] + at, 0]
-        n1 = nbr_ref[s_ref[1] + at, 1]
+        at = first_at + g
+        n0 = nbr_ref[at, 0]
+        n1 = nbr_ref[at, 1]
         lhs = jnp.where(low32, x_ref[n0].astype(F32), x_ref[n1].astype(F32)).astype(BF)
-        pair = dot(lhs, stage_ref[at]).astype(BF)
+        pair = dot(lhs, stage_ref[step * GROUP + g]).astype(BF)
         own = c_ref[pl.ds(pl.multiple_of(at * ORBS, ORBS), ORBS), :].astype(F32)
         sign = jnp.where(lax.broadcasted_iota(jnp.int32, own.shape, 1) < BANDS, 1.0, -1.0)
         first = (own * sign).astype(BF)
@@ -182,59 +168,62 @@
                         q * 16 + s * 8 : q * 16 + s * 8 + 8, e * 128 : e * 128 + 128
                     ]
 
-    rows = pl.ds(pl.multiple_of(step * GROUP_AUX, GROUP_AUX), GROUP_AUX)
+    rows = pl.ds(pl.multiple_of(first_at * AUX_ATOM, GROUP_AUX), GROUP_AUX)
     for l in range(OCC):
         out_ref[l, rows, :] = p_ref[l * PITCH : l * PITCH + GROUP_AUX, :].astype(BF)
 
 
-def pair_products(first, row, nbr, x, triple, coef, into=None, mib=24):
-    count = triple.shape[0]
-    extra = () if into is None else (into,)
-
-    def kernel(s_ref, nbr_ref, x_ref, triple_ref, c_ref, *rest):
+def pair_products(first, nbr, x, triples, coef, into=None, after=None, mib=24):
+    count = sum(t.shape[0] for t in triples)
+    m = len(triples)
+    extra = () if into is None else (into, after)
+
+    def kernel(s_ref, nbr_ref, x_ref, *rest):
+        triple_refs, coef_ref, rest = rest[:m], rest[m], rest[m + 1 :]
         if extra:
-            pair_kernel(s_ref, nbr_ref, None, x_ref, triple_ref, c_ref, *rest[len(extra) :])
+            pair_kernel(s_ref, nbr_ref, None, x_ref, triple_refs, coef_ref, *rest[2:])
         else:
-            out_ref, made_ref, *scratch = rest
-            pair_kernel(s_ref, nbr_ref, x_ref, made_ref, triple_ref, c_ref, out_ref, *scratch)
+            out_ref, made_ref, done_ref, *scratch = rest
+            done_ref[...] = jnp.zeros_like(done_ref)
+            pair_kernel(s_ref, nbr_ref, x_ref, made_ref, triple_refs, coef_ref, out_ref, *scratch)
 
     vmem = pl.BlockSpec(memory_space=pltpu.VMEM)
     out_shape = jax.ShapeDtypeStruct((OCC, NAUX, 128), BF)
     out_spec = pl.BlockSpec((OCC, count * AUX_ATOM, 128), lambda i, s, _: (0, s[0] // count, 0))
     made = jax.ShapeDtypeStruct((ATOMS, 2 * OCC, 128), BF)
+    token = jax.ShapeDtypeStruct((8, 128), F32)
     return pl.pallas_call(
         kernel,
-        out_shape=out_shape if extra else (out_shape, made),
+        out_shape=out_shape if extra else (out_shape, made, token),
         grid_spec=pltpu.PrefetchScalarGridSpec(
             num_scalar_prefetch=2,
             grid=(count // GROUP,),
             in_specs=[
                 whole(made.shape) if extra else vmem,
-                pl.BlockSpec(memory_space=pltpu.HBM),
-                pl.BlockSpec(memory_space=pltpu.HBM),
+                *(pl.BlockSpec(memory_space=pltpu.HBM) for _ in (*triples, coef)),
                 *(pl.BlockSpec(memory_space=pl.ANY) for _ in extra),
             ],
-            out_specs=out_spec if extra else (out_spec, whole(made.shape)),
+            out_specs=out_spec if extra else (out_spec, whole(made.shape), whole(token.shape)),
             scratch_shapes=[
-                pltpu.VMEM(triple.shape, BF),
+                pltpu.VMEM((count, *triples[0].shape[1:]), BF),
                 pltpu.VMEM((count * ORBS, 128), BF),
                 pltpu.VMEM((GROUP, 256, 256), BF),
                 pltpu.VMEM((OCC * PITCH + 8, 128), F32),
                 pltpu.SemaphoreType.DMA((count // GROUP + 1,)),
             ],
         ),
-        input_output_aliases={5: 0} if extra else {},
+        input_output_aliases={m + 4: 0} if extra else {},
         compiler_params=params(mib),
         cost_estimate=pl.CostEstimate(
             flops=count * 200_000_000, bytes_accessed=count * 250_000, transcendentals=0
         ),
         name="pair_products",
-    )(jnp.stack([first, row]), nbr, x, triple, coef, *extra)
+    )(first[None], nbr, x, *triples, coef, *extra)
 
 
 BLK = 256
 NB = NAUX // BLK
-BATCH = 4
+BATCH = 8
 
 
 def sigma_kernel(s_ref, p_ref, wa_ref, wb_ref, keep_ref, send_ref, re_ref, im_ref, acc_ref, sig_ref):
@@ -356,25 +345,17 @@
 
     smem = pl.BlockSpec(memory_space=pltpu.SMEM)
     vmem = pl.BlockSpec(memory_space=pltpu.VMEM)
-    hbm = pl.BlockSpec(memory_space=pl.ANY)
-    shared = (share, *triple.shape[1:])
-    pieces, sent = pl.pallas_call(
+    pieces = pl.pallas_call(
         pack_kernel,
-        out_shape=(
-            jax.ShapeDtypeStruct((PEERS * PIECE, 128), BF),
-            jax.ShapeDtypeStruct(shared, BF),
-        ),
-        in_specs=[smem, vmem, vmem, hbm],
-        out_specs=(vmem, hbm),
-        scratch_shapes=[
-            pltpu.VMEM(shared, BF),
-            pltpu.SemaphoreType.DMA((4,)),
-            pltpu.SemaphoreType.DMA((4,)),
-        ],
+        out_shape=jax.ShapeDtypeStruct((PEERS * PIECE, 128), BF),
+        in_specs=[smem, vmem, vmem],
+        out_specs=vmem,
         compiler_params=params(56),
         name="pack",
-    )(jnp.stack([h, core]), coef, w_screened[0], triple)
-    crossed = lax.ppermute(sent, (*KA, "aux"), x_crossing())
+    )(h[None], coef, w_screened[0])
+    crossed = lax.ppermute(
+        lax.dynamic_slice_in_dim(triple, core * share, share), (*KA, "aux"), x_crossing()
+    )
 
     spread = lax.all_to_all(
         pieces.reshape(PEERS, PIECE // 2, 2, 128), BY_CORE, split_axis=0, concat_axis=0, tiled=True
@@ -399,17 +380,21 @@
     )(h[None], partner_here, spread, own_piece(h), got)
     arrived = lax.all_to_all(routed, BY_CORE, split_axis=0, concat_axis=0, tiled=True)
 
-    crossed, arrived = lax.optimization_barrier((crossed, arrived))
+    here = arrived[:, split:].reshape(PACKED, 128)
+    far = arrived[:, :split].reshape(FAR, 128)
+    here, far = lax.optimization_barrier((here, far))
+    there = lax.ppermute(here, "core", swap)
+    others = (1 - h) * atoms
+    products, x, own_done = pair_products(h * atoms, neighbors, far, [triple], coef, mib=OWN_MIB)
+    crossed, own_done = lax.optimization_barrier((crossed, own_done))
     crossed2 = lax.ppermute(crossed, "core", swap)
-    here = arrived[:, split:].reshape(PACKED, 128)
-    there = lax.ppermute(here, "core", swap)
-    far = arrived.reshape(PEERS * PIECE, 128)
-    zero = jnp.zeros_like(h)
-    others = (1 - h) * atoms
-    products, x = pair_products(h * atoms, zero, neighbors, far, triple, coef, mib=OWN_MIB)
     near, away = core * share, (1 - core) * share
-    products = pair_products(others + near, near, nbr_other, x, crossed, coef, products)
-    products = pair_products(others + away, away, nbr_other, x, crossed2, coef, products)
+    products = pair_products(
+        others + near, lax.dynamic_slice_in_dim(nbr_other, near, share), x, [crossed], coef, products, own_done
+    )
+    products = pair_products(
+        others + away, lax.dynamic_slice_in_dim(nbr_other, away, share), x, [crossed2], coef, products, own_done
+    )
     keep, send = screened_sigma(h, core, products, here, there)
     return (keep + lax.ppermute(send, "aux", swap))[None]
 

time: 125 us -> 119 us (0.952)
  waiting for transfers between devices: 54.2 us -> 43.4 us
  local copies, waits for them, and re-layouts: 1.48 us -> 10.6 us
  Pallas kernels: 32.1 us -> 28.5 us
    ppermute x1, waiting for transfers between devices: 31.8 us -> 0.01 us  [local(): lax.ppermute(lax.dynamic_slice_in_dim(triple, core * share, share), (*KA,...]
    all_to_all x1, waiting for transfers between devices: 0.01 us -> 26 us  [local(): lax.all_to_all(routed, BY_CORE, split_axis=0, concat_axis=0, tiled=True)]
    unnamed x11 -> x17, local copies, waits for them, and re-layouts: 0.11 us -> 4.37 us
    dynamic_slice x0 -> x2, local copies, waits for them, and re-layouts: none -> 3.88 us  [the longest x1 3.88 us: local(): lax.dynamic_slice_in_dim(triple, core * share, share)]
    all_to_all x1, waiting for transfers between devices: 14.4 us -> 10.6 us  [local(): lax.all_to_all(pieces.reshape(PEERS, PIECE // 2, 2, 128), BY_CORE, split_...]
    pallas_call x1, Pallas kernels: 5.42 us -> 3.5 us  [local(): pl.pallas_call(pack_kernel, out_shape=jax.ShapeDtypeStruct((PEERS * PIECE...]
    pallas_call x1, Pallas kernels: 7.7 us -> 6.31 us  [screened_sigma(): pl.pallas_call(sigma_kernel, out_shape=(part, part), grid=(OCC // BATCH,)...]
  transfers between devices with their start and end apart: 8 -> 8, of which waited for: 5 -> 5; matrix products, arithmetic and copies ran while one was open for 1% -> 5% of each run, Pallas kernels for 15% -> 16%
where the time goes in v3:
time: 119 us
  waiting for transfers between devices  43.4 us (36%)
  starting transfers between devices  31.4 us (26%)
  Pallas kernels  28.5 us (24%)
  local copies, waits for them, and re-layouts  10.6 us (9%)
  between operations  3.88 us (3%)
    all_to_all x1, waiting for transfers between devices, local(): lax.all_to_all(routed, BY_CORE, split_axis=0, concat_axis=0, tiled=True)  26 us
    pallas_call x3, Pallas kernels, pair_products(): pl.pallas_call(kernel, out_shape=out_shape if extra else (out_shape, made...  16.9 us
    all_to_all x1, starting transfers between devices, local(): lax.all_to_all(pieces.reshape(PEERS, PIECE // 2, 2, 128), BY_CORE, split_...  15.2 us
    all_to_all x1, waiting for transfers between devices, local(): lax.all_to_all(pieces.reshape(PEERS, PIECE // 2, 2, 128), BY_CORE, split_...  10.6 us
    all_to_all x1, starting transfers between devices, local(): lax.all_to_all(routed, BY_CORE, split_axis=0, concat_axis=0, tiled=True)  7.24 us
    pallas_call x1, Pallas kernels, screened_sigma(): pl.pallas_call(sigma_kernel, out_shape=(part, part), grid=(OCC // BATCH,)...  6.31 us
    unnamed x17, local copies, waits for them, and re-layouts  4.37 us
    dynamic_slice x1, local copies, waits for them, and re-layouts, local(): lax.dynamic_slice_in_dim(triple, core * share, share)  3.88 us
  transfers between devices with their start and end apart: 8, of which 5 were waited for; matrix products, arithmetic and copies ran while one was open for 5% of the time, Pallas kernels for 16%

profile of v3, /device:TPU:1, one launch (start us, length us, event | category | flops | bytes accessed | tf_op | source)
XLA Modules:
  0.0 118.6 jit_solution(11982020788328014881)
XLA Ops:
  0.0 0.0 copy-start
  0.0 3.5 %pack.1 = bf16[3328,128]{1,0:T(8,128)(2,1)} custom-call(s32[1]{0:T(128)} %bitcast.h_ref, bf16[4096,128]{1,0:T(8,128)(2,1)} %bitcast.19, bf16[384,1536]{1,0:T(8,128)(2,1)} %bitcast.27), custom_call_target="tpu_custom_call" | custom-call | tf_op jit(solution)/shard_map/pack/pallas_call | solution.py:348
  3.5 15.2 %all-to-all-start = ((bf16[128,13,2,128]{3,2,1,0:T(2,128)(2,1)}), bf16[128,13,2,128]{3,2,1,0:T(2,128)(2,1)S(1)}, u32[]{:S(2)}, u32[]{:S(2)}) async-start(bf16[128,13,2,128]{3,2,1,0:T(2,128)(2,1)} %bitcast.24), calls=%async_computation | async-start | bytes 1703936 | tf_op jit(solution)/shard_map/all_to_all | solution.py:360
  18.7 0.0 copy-start.6
  18.7 0.0 copy-start.7
  18.7 3.9 %constant_dynamic-slice_fusion.1 = bf16[16,128,768]{2,1,0:T(8,128)(2,1)} fusion(bf16[32,128,768]{2,1,0:T(8,128)(2,1)} %bitcast.25, s32[]{:T(128)S(6)} %select_n.54), kind=kLoop, calls=%fused_computation.17 | loop fusion | bytes 6291460 | tf_op jit(solution)/shard_map/dynamic_slice | solution.py:357
  22.6 2.6 %collective-permute-start.2 = (bf16[16,128,768]{2,1,0:T(8,128)(2,1)}, bf16[16,128,768]{2,1,0:T(8,128)(2,1)}, u32[]{:S(2)}, u32[]{:S(2)}) collective-permute-start(bf16[16,128,768]{2,1,0:T(8,128)(2,1)} %constant_dynamic-slice_fusion.1), channel_id=1, source_target_pairs={{0,17},{1,16},{2,19},{3,18},{4,21},{5,20},{6,23},{7,22},{8,25},{9,... | collective-permute-start | bytes 9437192 | tf_op jit(solution)/shard_map/ppermute | solution.py:356
  25.3 0.0 copy-done.6
  25.3 0.1 copy.13.nbr_ref
  25.3 0.5 collective-permute-start
  25.9 0.0 copy-done
  25.9 0.1 squeeze.15
  26.1 0.1 copy.12
  26.2 0.1 reshape.17.partner_ref
  26.2 0.0 copy-done.7
  26.3 3.5 %collective-permute-done = s32[32,2]{1,0:T(8,128)S(1)} collective-permute-done((s32[32,2]{1,0:T(8,128)S(1)}, s32[32,2]{1,0:T(8,128)S(1)}, u32[]{:S(2)}, u32[]{:S(2)}) %collective-permute-start) | collective-permute-done | bytes 288 | tf_op jit(solution)/shard_map/ppermute | solution.py:344
  29.8 0.7 fusion.10
  34.2 10.6 %all-to-all-done.r_ref = bf16[128,13,2,128]{3,2,1,0:T(2,128)(2,1)S(1)} async-done(((bf16[128,13,2,128]{3,2,1,0:T(2,128)(2,1)}), bf16[128,13,2,128]{3,2,1,0:T(2,128)(2,1)S(1)}, u32[]{:S(2)}, u32[]{:S(2)}) %all-to-all-start) | async-done | bytes 852000 | tf_op jit(solution)/shard_map/all_to_all | solution.py:360
  44.8 2.5 %collective-permute-start.1 = (bf16[1,9,2,128]{3,2,1,0:T(2,128)(2,1)S(1)}, bf16[1,9,2,128]{3,2,1,0:T(2,128)(2,1)S(1)}, u32[]{:S(2)}, u32[]{:S(2)}) collective-permute-start(bf16[1,9,2,128]{3,2,1,0:T(2,128)(2,1)S(1)} %get-tuple-element.29), channel_id=1, source_target_pairs={{0,1},{1,0},{2,3},{3,2},{4,5},{5,4},{6,7},{7,6},{8,9},{9,8},{10,11... | collective-permute-start | bytes 13832 | tf_op jit(solution)/shard_map/ppermute | solution.py:372
  47.3 1.6 %collective-permute-done.1.got_ref = bf16[1,9,2,128]{3,2,1,0:T(2,128)(2,1)S(1)} collective-permute-done((bf16[1,9,2,128]{3,2,1,0:T(2,128)(2,1)S(1)}, bf16[1,9,2,128]{3,2,1,0:T(2,128)(2,1)S(1)}, u32[]{:S(2)}, u32[]{:S(2)}) %collective-permute-start.1) | collective-permute-done | bytes 4640 | tf_op jit(solution)/shard_map/ppermute | solution.py:372
  48.9 1.9 %route.1 = bf16[128,13,2,128]{3,2,1,0:T(2,128)(2,1)} custom-call(s32[1]{0:T(128)} %bitcast.h_ref, s32[128]{0:T(128)S(1)} %reshape.17.partner_ref, bf16[128,13,2,128]{3,2,1,0:T(2,128)(2,1)S(1)} %all-to-all-done.r_ref, bf16[1,9,2,128]{3,2,1,0:T(2,128)(2,1)S(1)} %get-tuple-element.30.own_ref, bf16[1,9,2,128]{3,2,1,0:T(2,128)(2,1)S(1)} %collective-permute-done.1.got_ref), custom_call_target="tpu_custom_call" | custom-call | tf_op jit(solution)/shard_map/route/pallas_call | solution.py:373
  50.8 7.2 %all-to-all-start.1 = ((bf16[128,13,2,128]{3,2,1,0:T(2,128)(2,1)}), bf16[128,13,2,128]{3,2,1,0:T(2,128)(2,1)S(1)}, u32[]{:S(2)}, u32[]{:S(2)}) async-start(bf16[128,13,2,128]{3,2,1,0:T(2,128)(2,1)} %route.1), calls=%async_computation.1 | async-start | bytes 1703936 | tf_op jit(solution)/shard_map/all_to_all | solution.py:381
  58.0 26.0 %all-to-all-done.1 = bf16[128,13,2,128]{3,2,1,0:T(2,128)(2,1)S(1)} async-done(((bf16[128,13,2,128]{3,2,1,0:T(2,128)(2,1)}), bf16[128,13,2,128]{3,2,1,0:T(2,128)(2,1)S(1)}, u32[]{:S(2)}, u32[]{:S(2)}) %all-to-all-start.1) | async-done | bytes 852000 | tf_op jit(solution)/shard_map/all_to_all | solution.py:381
  84.1 1.2 %slice.8 = bf16[128,9,2,128]{3,2,1,0:T(2,128)(2,1)} slice(bf16[128,13,2,128]{3,2,1,0:T(2,128)(2,1)S(1)} %all-to-all-done.1), slice={[0:128], [4:13], [0:2], [0:128]} | slice | bytes 1179648 | tf_op jit(solution)/shard_map/slice | solution.py:383
  85.3 0.2 slice.9
  85.5 0.0 copy-start.2
  85.5 1.2 %copy-done.2 = bf16[1,4096,128]{2,1,0:T(8,128)(2,1)S(1)} copy-done((bf16[1,4096,128]{2,1,0:T(8,128)(2,1)S(1)}, bf16[1,4096,128]{2,1,0:T(8,128)(2,1)}, u32[]{:S(2)}) %copy-start.2) | copy-done | bytes 1048600
  86.7 7.4 %pair_products.3 = (bf16[16,768,128]{2,1,0:T(8,128)(2,1)S(1)}, bf16[64,32,128]{2,1,0:T(8,128)(2,1)S(1)}, f32[8,128]{1,0:T(8,128)S(1)}) custom-call(s32[1]{0:T(128)} %bitcast.4.s_ref, s32[32,2]{1,0:T(8,128)S(1)} %copy.13.nbr_ref, bf16[1024,128]{1,0:T(8,128)(2,1)S(1)} %bitcast.23, bf16[32,128,768]{2,1,0:T(8,128)(2,1)} %bitcast.26, bf16[4096,128]{1,0:T(8,128)(2,1)S(1)} %bitcast.20), custom_call_target="tpu_custom_call" | custom-call | flops 6400000000 | bytes 8000000 | tf_op jit(solution)/shard_map/pair_products/pallas_call | solution.py:195
  94.2 0.0 copy-start.4
  94.2 0.8 copy-done.4
  95.0 0.0 collective-permute-done.2.rest_0_
  95.0 0.4 collective-permute-start.3
  95.4 0.1 pad_add_fusion.s_ref
  95.4 0.3 collective-permute-start.4
  95.8 0.0 copy-start.3
  95.8 1.2 %copy-done.3 = bf16[1,4096,128]{2,1,0:T(8,128)(2,1)S(1)} copy-done((bf16[1,4096,128]{2,1,0:T(8,128)(2,1)S(1)}, bf16[1,4096,128]{2,1,0:T(8,128)(2,1)}, u32[]{:S(2)}) %copy-start.3) | copy-done | bytes 1048600
  97.0 0.0 copy-start.5
  97.0 1.0 copy-done.5
  98.0 4.7 %pair_products.4.rest_2_ = bf16[16,768,128]{2,1,0:T(8,128)(2,1)S(1)} custom-call(s32[1]{0:T(128)} %bitcast.13.s_ref, s32[16,2]{1,0:T(8,128)S(1)} %get-tuple-element.31.nbr_ref, bf16[64,32,128]{2,1,0:T(8,128)(2,1)S(1)} %copy-done.5, bf16[16,128,768]{2,1,0:T(8,128)(2,1)} %collective-permute-done.2.rest_0_, ...), custom_call_target="tpu_custom_call", output_to_operand_aliasing={{}: (5, {})} | custom-call | flops 3200000000 | bytes 4000000 | tf_op jit(solution)/shard_map/pair_products/pallas_call | solution.py:195
  102.7 0.0 collective-permute-done.3.rest_0_
  102.8 0.0 copy-start.1
  102.8 4.7 %pair_products.5.p_ref = bf16[16,768,128]{2,1,0:T(8,128)(2,1)S(1)} custom-call(s32[1]{0:T(128)} %bitcast.2.s_ref, s32[16,2]{1,0:T(8,128)S(1)} %get-tuple-element.32.nbr_ref, bf16[64,32,128]{2,1,0:T(8,128)(2,1)S(1)} %copy-done.5, bf16[16,128,768]{2,1,0:T(8,128)(2,1)} %collective-permute-done.3.rest_0_, ...), custom_call_target="tpu_custom_call", output_to_operand_aliasing={{}: (5, {})} | custom-call | flops 3200000000 | bytes 4000000 | tf_op jit(solution)/shard_map/pair_products/pallas_call | solution.py:195
  107.5 0.0 collective-permute-done.4.wb_ref
  107.5 0.0 copy-done.1
  107.5 6.3 %screened_sigma.1 = (f32[32,128]{1,0:T(8,128)S(1)}, f32[32,128]{1,0:T(8,128)S(1)}) custom-call(s32[2]{0:T(128)S(1)} %pad_add_fusion.s_ref, bf16[16,768,128]{2,1,0:T(8,128)(2,1)S(1)} %pair_products.5.p_ref, bf16[2304,128]{1,0:T(8,128)(2,1)S(1)} %bitcast.18, bf16[2304,128]{1,0:T(8,128)(2,1)S(1)} %collective-permute-done.4.wb_ref), custom_call_target="tpu_custom_call" | custom-call | tf_op jit(solution)/shard_map/screened_sigma/pallas_call | solution.py:288
  113.8 2.5 %collective-permute-start.5 = (f32[32,128]{1,0:T(8,128)S(1)}, f32[32,128]{1,0:T(8,128)S(1)}, u32[]{:S(2)}, u32[]{:S(2)}) collective-permute-start(f32[32,128]{1,0:T(8,128)S(1)} %get-tuple-element.28), channel_id=1, source_target_pairs={{0,1},{1,0},{2,3},{3,2},{4,5},{5,4},{6,7},{7,6},{8,9},{9,8},{10,11... | collective-permute-start | bytes 49160 | tf_op jit(solution)/shard_map/ppermute | solution.py:399
  116.4 1.6 %collective-permute-done.5 = f32[32,128]{1,0:T(8,128)S(1)} collective-permute-done((f32[32,128]{1,0:T(8,128)S(1)}, f32[32,128]{1,0:T(8,128)S(1)}, u32[]{:S(2)}, u32[]{:S(2)}) %collective-permute-start.5) | collective-permute-done | bytes 16416 | tf_op jit(solution)/shard_map/ppermute | solution.py:399
  118.0 0.6 add_bitcast_fusion
  (5 shorter events, 0.1 us)
Async XLA Ops:
  0.0 25.9 %copy-start = (s32[2,128]{1,0:T(2,128)S(1)}, s32[2,128]{1,0:T(2,128)}, u32[]{:S(2)}) copy-start(s32[2,128]{1,0:T(2,128)} %param.10) | copy-start | bytes 3076
  3.5 41.2 %all-to-all-start = ((bf16[128,13,2,128]{3,2,1,0:T(2,128)(2,1)}), bf16[128,13,2,128]{3,2,1,0:T(2,128)(2,1)S(1)}, u32[]{:S(2)}, u32[]{:S(2)}) async-start(bf16[128,13,2,128]{3,2,1,0:T(2,128)(2,1)} %bitcast.24), calls=%async_computation | async-start | bytes 1703936 | tf_op jit(solution)/shard_map/all_to_all | solution.py:360
  18.7 6.6 %copy-start.6 = (s32[32,2]{0,1:T(2,128)S(1)}, s32[32,2]{0,1:T(2,128)}, u32[]{:S(2)}) copy-start(s32[32,2]{0,1:T(2,128)} %param.8) | copy-start | bytes 772
  18.7 7.5 %copy-start.7 = (s32[2]{0:T(128)S(1)}, s32[2]{0:T(128)}, u32[]{:S(2)}) copy-start(s32[2]{0:T(128)} %param.11) | copy-start | bytes 28
  22.6 72.4 %collective-permute-start.2 = (bf16[16,128,768]{2,1,0:T(8,128)(2,1)}, bf16[16,128,768]{2,1,0:T(8,128)(2,1)}, u32[]{:S(2)}, u32[]{:S(2)}) collective-permute-start(bf16[16,128,768]{2,1,0:T(8,128)(2,1)} %constant_dynamic-slice_fusion.1), channel_id=1, source_target_pairs={{0,17},{1,16},{2,19},{3,18},{4,21},{5,20},{6,23},{7,22},{8,25},{9,... | collective-permute-start | bytes 9437192 | tf_op jit(solution)/shard_map/ppermute | solution.py:356
  25.3 4.5 %collective-permute-start = (s32[32,2]{1,0:T(8,128)S(1)}, s32[32,2]{1,0:T(8,128)S(1)}, u32[]{:S(2)}, u32[]{:S(2)}) collective-permute-start(s32[32,2]{1,0:T(8,128)S(1)} %copy.13.nbr_ref), channel_id=1, source_target_pairs={{0,1},{1,0},{2,3},{3,2},{4,5},{5,4},{6,7},{7,6},{8,9},{9,8},{10,11... | collective-permute-start | bytes 776 | tf_op jit(solution)/shard_map/ppermute | solution.py:344
  44.8 4.2 %collective-permute-start.1 = (bf16[1,9,2,128]{3,2,1,0:T(2,128)(2,1)S(1)}, bf16[1,9,2,128]{3,2,1,0:T(2,128)(2,1)S(1)}, u32[]{:S(2)}, u32[]{:S(2)}) collective-permute-start(bf16[1,9,2,128]{3,2,1,0:T(2,128)(2,1)S(1)} %get-tuple-element.29), channel_id=1, source_target_pairs={{0,1},{1,0},{2,3},{3,2},{4,5},{5,4},{6,7},{7,6},{8,9},{9,8},{10,11... | collective-permute-start | bytes 13832 | tf_op jit(solution)/shard_map/ppermute | solution.py:372
  50.8 33.3 %all-to-all-start.1 = ((bf16[128,13,2,128]{3,2,1,0:T(2,128)(2,1)}), bf16[128,13,2,128]{3,2,1,0:T(2,128)(2,1)S(1)}, u32[]{:S(2)}, u32[]{:S(2)}) async-start(bf16[128,13,2,128]{3,2,1,0:T(2,128)(2,1)} %route.1), calls=%async_computation.1 | async-start | bytes 1703936 | tf_op jit(solution)/shard_map/all_to_all | solution.py:381
  85.5 1.2 %copy-start.2 = (bf16[1,4096,128]{2,1,0:T(8,128)(2,1)S(1)}, bf16[1,4096,128]{2,1,0:T(8,128)(2,1)}, u32[]{:S(2)}) copy-start(bf16[1,4096,128]{2,1,0:T(8,128)(2,1)} %param.6) | copy-start | bytes 3145732
  94.2 0.8 copy-start.4
  95.0 7.8 %collective-permute-start.3 = (bf16[16,128,768]{2,1,0:T(8,128)(2,1)}, bf16[16,128,768]{2,1,0:T(8,128)(2,1)}, u32[]{:S(2)}, u32[]{:S(2)}) collective-permute-start(bf16[16,128,768]{2,1,0:T(8,128)(2,1)} %collective-permute-done.2.rest_0_), channel_id=1, source_target_pairs={{0,2},{2,0},{1,3},{3,1},{4,6},{6,4},{5,7},{7,5},{8,10},{10,8},{9,1... | collective-permute-start | bytes 9437192 | tf_op jit(solution)/shard_map/ppermute | solution.py:390
  95.4 12.1 %collective-permute-start.4 = (bf16[2304,128]{1,0:T(8,128)(2,1)}, bf16[2304,128]{1,0:T(8,128)(2,1)S(1)}, u32[]{:S(2)}, u32[]{:S(2)}) collective-permute-start(bf16[2304,128]{1,0:T(8,128)(2,1)} %bitcast.17), channel_id=1, source_target_pairs={{0,2},{2,0},{1,3},{3,1},{4,6},{6,4},{5,7},{7,5},{8,10},{10,8},{9,1... | collective-permute-start | bytes 1769480 | tf_op jit(solution)/shard_map/ppermute | solution.py:386
  95.8 1.2 %copy-start.3 = (bf16[1,4096,128]{2,1,0:T(8,128)(2,1)S(1)}, bf16[1,4096,128]{2,1,0:T(8,128)(2,1)}, u32[]{:S(2)}) copy-start(bf16[1,4096,128]{2,1,0:T(8,128)(2,1)} %param.6) | copy-start | bytes 3145732
  97.0 1.0 copy-start.5
  102.8 4.7 %copy-start.1 = (bf16[128,9,2,128]{3,2,1,0:T(2,128)(2,1)S(1)}, bf16[128,9,2,128]{3,2,1,0:T(2,128)(2,1)}, u32[]{:S(2)}) copy-start(bf16[128,9,2,128]{3,2,1,0:T(2,128)(2,1)} %slice.8) | copy-start | bytes 1769476
  113.8 4.2 %collective-permute-start.5 = (f32[32,128]{1,0:T(8,128)S(1)}, f32[32,128]{1,0:T(8,128)S(1)}, u32[]{:S(2)}, u32[]{:S(2)}) collective-permute-start(f32[32,128]{1,0:T(8,128)S(1)} %get-tuple-element.28), channel_id=1, source_target_pairs={{0,1},{1,0},{2,3},{3,2},{4,5},{5,4},{6,7},{7,6},{8,9},{9,8},{10,11... | collective-permute-start | bytes 49160 | tf_op jit(solution)/shard_map/ppermute | solution.py:399

commit v4 on v3

--- a/solution.py
+++ b/solution.py
@@ -75,6 +75,24 @@
                 a = b
 
 
+def share_kernel(first_ref, triple_ref, out_ref, stage_ref, in_sem, out_sem):
+    parts = in_sem.shape[0]
+    size = out_ref.shape[0] // parts
+    reads, writes = [], []
+    for n in range(parts):
+        rows = pl.ds(n * size, size)
+        source = triple_ref.at[pl.ds(first_ref[0] + n * size, size)]
+        reads.append(pltpu.make_async_copy(source, stage_ref.at[rows], in_sem.at[n]))
+        writes.append(pltpu.make_async_copy(stage_ref.at[rows], out_ref.at[rows], out_sem.at[n]))
+    for copy in reads:
+        copy.start()
+    for read, write in zip(reads, writes):
+        read.wait()
+        write.start()
+    for copy in writes:
+        copy.wait()
+
+
 def route_kernel(h_ref, partner_ref, r_ref, own_ref, got_ref, out_ref):
     split = FAR_ROWS // 2
     first = h_ref[0] == 0
@@ -90,6 +108,7 @@
 
 
 OWN_MIB = 48
+OTHER_MIB = 24
 GROUP = 8
 GROUP_AUX = GROUP * AUX_ATOM
 PITCH = GROUP_AUX + 1
@@ -223,7 +242,7 @@
 
 BLK = 256
 NB = NAUX // BLK
-BATCH = 8
+BATCH = 16
 
 
 def sigma_kernel(s_ref, p_ref, wa_ref, wb_ref, keep_ref, send_ref, re_ref, im_ref, acc_ref, sig_ref):
@@ -353,9 +372,21 @@
         compiler_params=params(56),
         name="pack",
     )(h[None], coef, w_screened[0])
-    crossed = lax.ppermute(
-        lax.dynamic_slice_in_dim(triple, core * share, share), (*KA, "aux"), x_crossing()
-    )
+    shared = (share, *triple.shape[1:])
+    sent = pl.pallas_call(
+        share_kernel,
+        out_shape=jax.ShapeDtypeStruct(shared, BF),
+        in_specs=[smem, pl.BlockSpec(memory_space=pl.ANY)],
+        out_specs=pl.BlockSpec(memory_space=pl.ANY),
+        scratch_shapes=[
+            pltpu.VMEM(shared, BF),
+            pltpu.SemaphoreType.DMA((8,)),
+            pltpu.SemaphoreType.DMA((8,)),
+        ],
+        compiler_params=params(56),
+        name="share",
+    )((core * share)[None], triple)
+    crossed = lax.ppermute(sent, (*KA, "aux"), x_crossing())
 
     spread = lax.all_to_all(
         pieces.reshape(PEERS, PIECE // 2, 2, 128), BY_CORE, split_axis=0, concat_axis=0, tiled=True
@@ -390,10 +421,10 @@
     crossed2 = lax.ppermute(crossed, "core", swap)
     near, away = core * share, (1 - core) * share
     products = pair_products(
-        others + near, lax.dynamic_slice_in_dim(nbr_other, near, share), x, [crossed], coef, products, own_done
+        others + near, lax.dynamic_slice_in_dim(nbr_other, near, share), x, [crossed], coef, products, own_done, mib=OTHER_MIB
     )
     products = pair_products(
-        others + away, lax.dynamic_slice_in_dim(nbr_other, away, share), x, [crossed2], coef, products, own_done
+        others + away, lax.dynamic_slice_in_dim(nbr_other, away, share), x, [crossed2], coef, products, own_done, mib=OTHER_MIB
     )
     keep, send = screened_sigma(h, core, products, here, there)
     return (keep + lax.ppermute(send, "aux", swap))[None]

time: 119 us -> 119 us (level)
  local copies, waits for them, and re-layouts: 10.6 us -> 6.76 us
  Pallas kernels: 28.5 us -> 30.9 us
    dynamic_slice x1 -> x0, local copies, waits for them, and re-layouts: 3.88 us -> none  [local(): lax.dynamic_slice_in_dim(triple, core * share, share)]
    pallas_call x0 -> x1, Pallas kernels: none -> 2.85 us  [local(): pl.pallas_call(share_kernel, out_shape=jax.ShapeDtypeStruct(shared, BF),...]
  transfers between devices with their start and end apart: 8 -> 8, of which waited for: 5 -> 5; matrix products, arithmetic and copies ran while one was open for 5% -> 2% of each run, Pallas kernels for 16% -> 18%
where the time goes in v4:
time: 119 us; the launch traced here: 118 us
  waiting for transfers between devices  44.4 us (37%)
  starting transfers between devices  31.5 us (26%)
  Pallas kernels  30.9 us (26%)
  local copies, waits for them, and re-layouts  6.76 us (6%)
  between operations  3.89 us (3%)
    all_to_all x1, waiting for transfers between devices, local(): lax.all_to_all(routed, BY_CORE, split_axis=0, concat_axis=0, tiled=True)  26 us
    pallas_call x3, Pallas kernels, pair_products(): pl.pallas_call(kernel, out_shape=out_shape if extra else (out_shape, made...  16.9 us
    all_to_all x1, starting transfers between devices, local(): lax.all_to_all(pieces.reshape(PEERS, PIECE // 2, 2, 128), BY_CORE, split_...  15.2 us
    all_to_all x1, waiting for transfers between devices, local(): lax.all_to_all(pieces.reshape(PEERS, PIECE // 2, 2, 128), BY_CORE, split_...  11.5 us
    all_to_all x1, starting transfers between devices, local(): lax.all_to_all(routed, BY_CORE, split_axis=0, concat_axis=0, tiled=True)  7.24 us
    pallas_call x1, Pallas kernels, screened_sigma(): pl.pallas_call(sigma_kernel, out_shape=(part, part), grid=(OCC // BATCH,)...  5.81 us
    unnamed x17, local copies, waits for them, and re-layouts  4.37 us
    ppermute x1, waiting for transfers between devices, local(): nbr_other = lax.ppermute(neighbors, 'aux', swap)  3.54 us
  transfers between devices with their start and end apart: 8, of which 5 were waited for; matrix products, arithmetic and copies ran while one was open for 2% of the time, Pallas kernels for 18%

profile of v4, /device:TPU:1, one launch (start us, length us, event | category | flops | bytes accessed | tf_op | source)
XLA Modules:
  0.0 118.1 jit_solution(14997443859377092597)
XLA Ops:
  0.0 0.0 copy-start
  0.0 3.5 %pack.1 = bf16[3328,128]{1,0:T(8,128)(2,1)} custom-call(s32[1]{0:T(128)} %bitcast.h_ref, bf16[4096,128]{1,0:T(8,128)(2,1)} %bitcast.20, bf16[384,1536]{1,0:T(8,128)(2,1)} %bitcast.28), custom_call_target="tpu_custom_call" | custom-call | tf_op jit(solution)/shard_map/pack/pallas_call | solution.py:367
  3.5 15.2 %all-to-all-start = ((bf16[128,13,2,128]{3,2,1,0:T(2,128)(2,1)}), bf16[128,13,2,128]{3,2,1,0:T(2,128)(2,1)S(1)}, u32[]{:S(2)}, u32[]{:S(2)}) async-start(bf16[128,13,2,128]{3,2,1,0:T(2,128)(2,1)} %bitcast.27), calls=%async_computation | async-start | bytes 1703936 | tf_op jit(solution)/shard_map/all_to_all | solution.py:391
  18.7 0.0 copy-start.6
  18.7 0.0 copy-start.7
  18.7 2.8 %share.1 = bf16[16,128,768]{2,1,0:T(8,128)(2,1)} custom-call(s32[1]{0:T(128)} %bitcast.13.first_ref, bf16[32,128,768]{2,1,0:T(8,128)(2,1)} %bitcast.25), custom_call_target="tpu_custom_call" | custom-call | tf_op jit(solution)/shard_map/share/pallas_call | solution.py:376
  21.6 2.7 %collective-permute-start.2 = (bf16[16,128,768]{2,1,0:T(8,128)(2,1)}, bf16[16,128,768]{2,1,0:T(8,128)(2,1)}, u32[]{:S(2)}, u32[]{:S(2)}) collective-permute-start(bf16[16,128,768]{2,1,0:T(8,128)(2,1)} %share.1), channel_id=1, source_target_pairs={{0,17},{1,16},{2,19},{3,18},{4,21},{5,20},{6,23},{7,22},{8,25},{9,... | collective-permute-start | bytes 9437192 | tf_op jit(solution)/shard_map/ppermute | solution.py:389
  24.3 0.0 copy-done.6
  24.3 0.1 copy.13.nbr_ref
  24.4 0.5 collective-permute-start
  24.9 0.0 copy-done
  25.0 0.1 squeeze.15
  25.1 0.1 copy.12
  25.2 0.1 reshape.17.partner_ref
  25.3 0.0 copy-done.7
  25.3 3.5 %collective-permute-done = s32[32,2]{1,0:T(8,128)S(1)} collective-permute-done((s32[32,2]{1,0:T(8,128)S(1)}, s32[32,2]{1,0:T(8,128)S(1)}, u32[]{:S(2)}, u32[]{:S(2)}) %collective-permute-start) | collective-permute-done | bytes 288 | tf_op jit(solution)/shard_map/ppermute | solution.py:363
  28.9 0.7 fusion.10
  33.2 11.5 %all-to-all-done.r_ref = bf16[128,13,2,128]{3,2,1,0:T(2,128)(2,1)S(1)} async-done(((bf16[128,13,2,128]{3,2,1,0:T(2,128)(2,1)}), bf16[128,13,2,128]{3,2,1,0:T(2,128)(2,1)S(1)}, u32[]{:S(2)}, u32[]{:S(2)}) %all-to-all-start) | async-done | bytes 852000 | tf_op jit(solution)/shard_map/all_to_all | solution.py:391
  44.8 2.5 %collective-permute-start.1 = (bf16[1,9,2,128]{3,2,1,0:T(2,128)(2,1)S(1)}, bf16[1,9,2,128]{3,2,1,0:T(2,128)(2,1)S(1)}, u32[]{:S(2)}, u32[]{:S(2)}) collective-permute-start(bf16[1,9,2,128]{3,2,1,0:T(2,128)(2,1)S(1)} %get-tuple-element.29), channel_id=1, source_target_pairs={{0,1},{1,0},{2,3},{3,2},{4,5},{5,4},{6,7},{7,6},{8,9},{9,8},{10,11... | collective-permute-start | bytes 13832 | tf_op jit(solution)/shard_map/ppermute | solution.py:403
  47.3 1.6 %collective-permute-done.1.got_ref = bf16[1,9,2,128]{3,2,1,0:T(2,128)(2,1)S(1)} collective-permute-done((bf16[1,9,2,128]{3,2,1,0:T(2,128)(2,1)S(1)}, bf16[1,9,2,128]{3,2,1,0:T(2,128)(2,1)S(1)}, u32[]{:S(2)}, u32[]{:S(2)}) %collective-permute-start.1) | collective-permute-done | bytes 4640 | tf_op jit(solution)/shard_map/ppermute | solution.py:403
  48.9 1.9 %route.1 = bf16[128,13,2,128]{3,2,1,0:T(2,128)(2,1)} custom-call(s32[1]{0:T(128)} %bitcast.h_ref, s32[128]{0:T(128)S(1)} %reshape.17.partner_ref, bf16[128,13,2,128]{3,2,1,0:T(2,128)(2,1)S(1)} %all-to-all-done.r_ref, bf16[1,9,2,128]{3,2,1,0:T(2,128)(2,1)S(1)} %get-tuple-element.30.own_ref, bf16[1,9,2,128]{3,2,1,0:T(2,128)(2,1)S(1)} %collective-permute-done.1.got_ref), custom_call_target="tpu_custom_call" | custom-call | tf_op jit(solution)/shard_map/route/pallas_call | solution.py:404
  50.8 7.2 %all-to-all-start.1 = ((bf16[128,13,2,128]{3,2,1,0:T(2,128)(2,1)}), bf16[128,13,2,128]{3,2,1,0:T(2,128)(2,1)S(1)}, u32[]{:S(2)}, u32[]{:S(2)}) async-start(bf16[128,13,2,128]{3,2,1,0:T(2,128)(2,1)} %route.1), calls=%async_computation.1 | async-start | bytes 1703936 | tf_op jit(solution)/shard_map/all_to_all | solution.py:412
  58.0 26.0 %all-to-all-done.1 = bf16[128,13,2,128]{3,2,1,0:T(2,128)(2,1)S(1)} async-done(((bf16[128,13,2,128]{3,2,1,0:T(2,128)(2,1)}), bf16[128,13,2,128]{3,2,1,0:T(2,128)(2,1)S(1)}, u32[]{:S(2)}, u32[]{:S(2)}) %all-to-all-start.1) | async-done | bytes 852000 | tf_op jit(solution)/shard_map/all_to_all | solution.py:412
  84.1 1.2 %slice.8 = bf16[128,9,2,128]{3,2,1,0:T(2,128)(2,1)} slice(bf16[128,13,2,128]{3,2,1,0:T(2,128)(2,1)S(1)} %all-to-all-done.1), slice={[0:128], [4:13], [0:2], [0:128]} | slice | bytes 1179648 | tf_op jit(solution)/shard_map/slice | solution.py:414
  85.3 0.2 slice.9
  85.5 0.0 copy-start.2
  85.5 1.2 %copy-done.2 = bf16[1,4096,128]{2,1,0:T(8,128)(2,1)S(1)} copy-done((bf16[1,4096,128]{2,1,0:T(8,128)(2,1)S(1)}, bf16[1,4096,128]{2,1,0:T(8,128)(2,1)}, u32[]{:S(2)}) %copy-start.2) | copy-done | bytes 1048600
  86.7 7.4 %pair_products.3 = (bf16[16,768,128]{2,1,0:T(8,128)(2,1)S(1)}, bf16[64,32,128]{2,1,0:T(8,128)(2,1)S(1)}, f32[8,128]{1,0:T(8,128)S(1)}) custom-call(s32[1]{0:T(128)} %bitcast.4.s_ref, s32[32,2]{1,0:T(8,128)S(1)} %copy.13.nbr_ref, bf16[1024,128]{1,0:T(8,128)(2,1)S(1)} %bitcast.24, bf16[32,128,768]{2,1,0:T(8,128)(2,1)} %bitcast.26, bf16[4096,128]{1,0:T(8,128)(2,1)S(1)} %bitcast.21), custom_call_target="tpu_custom_call" | custom-call | flops 6400000000 | bytes 8000000 | tf_op jit(solution)/shard_map/pair_products/pallas_call | solution.py:214
  94.2 0.0 copy-start.4
  94.2 0.8 copy-done.4
  95.0 0.0 collective-permute-done.2.rest_0_
  95.0 0.4 collective-permute-start.3
  95.4 0.1 pad_add_fusion.s_ref
  95.4 0.3 collective-permute-start.4
  95.8 0.0 copy-start.3
  95.8 1.2 %copy-done.3 = bf16[1,4096,128]{2,1,0:T(8,128)(2,1)S(1)} copy-done((bf16[1,4096,128]{2,1,0:T(8,128)(2,1)S(1)}, bf16[1,4096,128]{2,1,0:T(8,128)(2,1)}, u32[]{:S(2)}) %copy-start.3) | copy-done | bytes 1048600
  97.0 0.0 copy-start.5
  97.0 1.0 copy-done.5
  98.0 4.7 %pair_products.4.rest_2_ = bf16[16,768,128]{2,1,0:T(8,128)(2,1)S(1)} custom-call(s32[1]{0:T(128)} %bitcast.14.s_ref, s32[16,2]{1,0:T(8,128)S(1)} %get-tuple-element.31.nbr_ref, bf16[64,32,128]{2,1,0:T(8,128)(2,1)S(1)} %copy-done.5, bf16[16,128,768]{2,1,0:T(8,128)(2,1)} %collective-permute-done.2.rest_0_, ...), custom_call_target="tpu_custom_call", output_to_operand_aliasing={{}: (5, {})} | custom-call | flops 3200000000 | bytes 4000000 | tf_op jit(solution)/shard_map/pair_products/pallas_call | solution.py:214
  102.8 0.0 collective-permute-done.3.rest_0_
  102.8 0.0 copy-start.1
  102.8 4.7 %pair_products.5.p_ref = bf16[16,768,128]{2,1,0:T(8,128)(2,1)S(1)} custom-call(s32[1]{0:T(128)} %bitcast.2.s_ref, s32[16,2]{1,0:T(8,128)S(1)} %get-tuple-element.32.nbr_ref, bf16[64,32,128]{2,1,0:T(8,128)(2,1)S(1)} %copy-done.5, bf16[16,128,768]{2,1,0:T(8,128)(2,1)} %collective-permute-done.3.rest_0_, ...), custom_call_target="tpu_custom_call", output_to_operand_aliasing={{}: (5, {})} | custom-call | flops 3200000000 | bytes 4000000 | tf_op jit(solution)/shard_map/pair_products/pallas_call | solution.py:214
  107.5 0.0 collective-permute-done.4.wb_ref
  107.5 0.0 copy-done.1
  107.5 5.8 %screened_sigma.1 = (f32[32,128]{1,0:T(8,128)S(1)}, f32[32,128]{1,0:T(8,128)S(1)}) custom-call(s32[2]{0:T(128)S(1)} %pad_add_fusion.s_ref, bf16[16,768,128]{2,1,0:T(8,128)(2,1)S(1)} %pair_products.5.p_ref, bf16[2304,128]{1,0:T(8,128)(2,1)S(1)} %bitcast.19, bf16[2304,128]{1,0:T(8,128)(2,1)S(1)} %collective-permute-done.4.wb_ref), custom_call_target="tpu_custom_call" | custom-call | tf_op jit(solution)/shard_map/screened_sigma/pallas_call | solution.py:307
  113.3 2.5 %collective-permute-start.5 = (f32[32,128]{1,0:T(8,128)S(1)}, f32[32,128]{1,0:T(8,128)S(1)}, u32[]{:S(2)}, u32[]{:S(2)}) collective-permute-start(f32[32,128]{1,0:T(8,128)S(1)} %get-tuple-element.28), channel_id=1, source_target_pairs={{0,1},{1,0},{2,3},{3,2},{4,5},{5,4},{6,7},{7,6},{8,9},{9,8},{10,11... | collective-permute-start | bytes 49160 | tf_op jit(solution)/shard_map/ppermute | solution.py:430
  115.9 1.6 %collective-permute-done.5 = f32[32,128]{1,0:T(8,128)S(1)} collective-permute-done((f32[32,128]{1,0:T(8,128)S(1)}, f32[32,128]{1,0:T(8,128)S(1)}, u32[]{:S(2)}, u32[]{:S(2)}) %collective-permute-start.5) | collective-permute-done | bytes 16416 | tf_op jit(solution)/shard_map/ppermute | solution.py:430
  117.5 0.6 add_bitcast_fusion
  (5 shorter events, 0.1 us)
Async XLA Ops:
  0.0 24.9 %copy-start = (s32[2,128]{1,0:T(2,128)S(1)}, s32[2,128]{1,0:T(2,128)}, u32[]{:S(2)}) copy-start(s32[2,128]{1,0:T(2,128)} %param.10) | copy-start | bytes 3076
  3.5 41.2 %all-to-all-start = ((bf16[128,13,2,128]{3,2,1,0:T(2,128)(2,1)}), bf16[128,13,2,128]{3,2,1,0:T(2,128)(2,1)S(1)}, u32[]{:S(2)}, u32[]{:S(2)}) async-start(bf16[128,13,2,128]{3,2,1,0:T(2,128)(2,1)} %bitcast.27), calls=%async_computation | async-start | bytes 1703936 | tf_op jit(solution)/shard_map/all_to_all | solution.py:391
  18.7 5.6 %copy-start.6 = (s32[32,2]{0,1:T(2,128)S(1)}, s32[32,2]{0,1:T(2,128)}, u32[]{:S(2)}) copy-start(s32[32,2]{0,1:T(2,128)} %param.8) | copy-start | bytes 772
  18.7 6.6 %copy-start.7 = (s32[2]{0:T(128)S(1)}, s32[2]{0:T(128)}, u32[]{:S(2)}) copy-start(s32[2]{0:T(128)} %param.11) | copy-start | bytes 28
  21.6 73.4 %collective-permute-start.2 = (bf16[16,128,768]{2,1,0:T(8,128)(2,1)}, bf16[16,128,768]{2,1,0:T(8,128)(2,1)}, u32[]{:S(2)}, u32[]{:S(2)}) collective-permute-start(bf16[16,128,768]{2,1,0:T(8,128)(2,1)} %share.1), channel_id=1, source_target_pairs={{0,17},{1,16},{2,19},{3,18},{4,21},{5,20},{6,23},{7,22},{8,25},{9,... | collective-permute-start | bytes 9437192 | tf_op jit(solution)/shard_map/ppermute | solution.py:389
  24.4 4.5 %collective-permute-start = (s32[32,2]{1,0:T(8,128)S(1)}, s32[32,2]{1,0:T(8,128)S(1)}, u32[]{:S(2)}, u32[]{:S(2)}) collective-permute-start(s32[32,2]{1,0:T(8,128)S(1)} %copy.13.nbr_ref), channel_id=1, source_target_pairs={{0,1},{1,0},{2,3},{3,2},{4,5},{5,4},{6,7},{7,6},{8,9},{9,8},{10,11... | collective-permute-start | bytes 776 | tf_op jit(solution)/shard_map/ppermute | solution.py:363
  44.8 4.2 %collective-permute-start.1 = (bf16[1,9,2,128]{3,2,1,0:T(2,128)(2,1)S(1)}, bf16[1,9,2,128]{3,2,1,0:T(2,128)(2,1)S(1)}, u32[]{:S(2)}, u32[]{:S(2)}) collective-permute-start(bf16[1,9,2,128]{3,2,1,0:T(2,128)(2,1)S(1)} %get-tuple-element.29), channel_id=1, source_target_pairs={{0,1},{1,0},{2,3},{3,2},{4,5},{5,4},{6,7},{7,6},{8,9},{9,8},{10,11... | collective-permute-start | bytes 13832 | tf_op jit(solution)/shard_map/ppermute | solution.py:403
  50.8 33.3 %all-to-all-start.1 = ((bf16[128,13,2,128]{3,2,1,0:T(2,128)(2,1)}), bf16[128,13,2,128]{3,2,1,0:T(2,128)(2,1)S(1)}, u32[]{:S(2)}, u32[]{:S(2)}) async-start(bf16[128,13,2,128]{3,2,1,0:T(2,128)(2,1)} %route.1), calls=%async_computation.1 | async-start | bytes 1703936 | tf_op jit(solution)/shard_map/all_to_all | solution.py:412
  85.5 1.2 %copy-start.2 = (bf16[1,4096,128]{2,1,0:T(8,128)(2,1)S(1)}, bf16[1,4096,128]{2,1,0:T(8,128)(2,1)}, u32[]{:S(2)}) copy-start(bf16[1,4096,128]{2,1,0:T(8,128)(2,1)} %param.6) | copy-start | bytes 3145732
  94.2 0.8 copy-start.4
  95.0 7.8 %collective-permute-start.3 = (bf16[16,128,768]{2,1,0:T(8,128)(2,1)}, bf16[16,128,768]{2,1,0:T(8,128)(2,1)}, u32[]{:S(2)}, u32[]{:S(2)}) collective-permute-start(bf16[16,128,768]{2,1,0:T(8,128)(2,1)} %collective-permute-done.2.rest_0_), channel_id=1, source_target_pairs={{0,2},{2,0},{1,3},{3,1},{4,6},{6,4},{5,7},{7,5},{8,10},{10,8},{9,1... | collective-permute-start | bytes 9437192 | tf_op jit(solution)/shard_map/ppermute | solution.py:421
  95.4 12.1 %collective-permute-start.4 = (bf16[2304,128]{1,0:T(8,128)(2,1)}, bf16[2304,128]{1,0:T(8,128)(2,1)S(1)}, u32[]{:S(2)}, u32[]{:S(2)}) collective-permute-start(bf16[2304,128]{1,0:T(8,128)(2,1)} %bitcast.18), channel_id=1, source_target_pairs={{0,2},{2,0},{1,3},{3,1},{4,6},{6,4},{5,7},{7,5},{8,10},{10,8},{9,1... | collective-permute-start | bytes 1769480 | tf_op jit(solution)/shard_map/ppermute | solution.py:417
  95.8 1.2 %copy-start.3 = (bf16[1,4096,128]{2,1,0:T(8,128)(2,1)S(1)}, bf16[1,4096,128]{2,1,0:T(8,128)(2,1)}, u32[]{:S(2)}) copy-start(bf16[1,4096,128]{2,1,0:T(8,128)(2,1)} %param.6) | copy-start | bytes 3145732
  97.0 1.0 copy-start.5
  102.8 4.7 %copy-start.1 = (bf16[128,9,2,128]{3,2,1,0:T(2,128)(2,1)S(1)}, bf16[128,9,2,128]{3,2,1,0:T(2,128)(2,1)}, u32[]{:S(2)}) copy-start(bf16[128,9,2,128]{3,2,1,0:T(2,128)(2,1)} %slice.8) | copy-start | bytes 1769476
  113.3 4.2 %collective-permute-start.5 = (f32[32,128]{1,0:T(8,128)S(1)}, f32[32,128]{1,0:T(8,128)S(1)}, u32[]{:S(2)}, u32[]{:S(2)}) collective-permute-start(f32[32,128]{1,0:T(8,128)S(1)} %get-tuple-element.28), channel_id=1, source_target_pairs={{0,1},{1,0},{2,3},{3,2},{4,5},{5,4},{6,7},{7,6},{8,9},{9,8},{10,11... | collective-permute-start | bytes 49160 | tf_op jit(solution)/shard_map/ppermute | solution.py:430

commit v5 on v4

--- a/solution.py
+++ b/solution.py
@@ -109,7 +109,7 @@
 
 OWN_MIB = 48
 OTHER_MIB = 24
-GROUP = 8
+GROUP = 4
 GROUP_AUX = GROUP * AUX_ATOM
 PITCH = GROUP_AUX + 1
 

time: 119 us -> 119 us (level)
  transfers between devices with their start and end apart: 8 -> 8, of which waited for: 5 -> 5; matrix products, arithmetic and copies ran while one was open for 2% -> 2% of each run, Pallas kernels for 18% -> 19%
where the time goes in v5:
time: 119 us
  waiting for transfers between devices  44.4 us (37%)
  Pallas kernels  31.7 us (27%)
  starting transfers between devices  31.5 us (26%)
  local copies, waits for them, and re-layouts  6.76 us (6%)
  between operations  3.89 us (3%)
    all_to_all x1, waiting for transfers between devices, local(): lax.all_to_all(routed, BY_CORE, split_axis=0, concat_axis=0, tiled=True)  26 us
    pallas_call x3, Pallas kernels, pair_products(): pl.pallas_call(kernel, out_shape=out_shape if extra else (out_shape, made...  17.6 us
    all_to_all x1, starting transfers between devices, local(): lax.all_to_all(pieces.reshape(PEERS, PIECE // 2, 2, 128), BY_CORE, split_...  15.2 us
    all_to_all x1, waiting for transfers between devices, local(): lax.all_to_all(pieces.reshape(PEERS, PIECE // 2, 2, 128), BY_CORE, split_...  11.5 us
    all_to_all x1, starting transfers between devices, local(): lax.all_to_all(routed, BY_CORE, split_axis=0, concat_axis=0, tiled=True)  7.24 us
    pallas_call x1, Pallas kernels, screened_sigma(): pl.pallas_call(sigma_kernel, out_shape=(part, part), grid=(OCC // BATCH,)...  5.81 us
    unnamed x17, local copies, waits for them, and re-layouts  4.37 us
    ppermute x1, waiting for transfers between devices, local(): nbr_other = lax.ppermute(neighbors, 'aux', swap)  3.54 us
  transfers between devices with their start and end apart: 8, of which 5 were waited for; matrix products, arithmetic and copies ran while one was open for 2% of the time, Pallas kernels for 19%

profile of v5, /device:TPU:1, one launch (start us, length us, event | category | flops | bytes accessed | tf_op | source)
XLA Modules:
  0.0 118.9 jit_solution(16097881208192251679)
XLA Ops:
  0.0 0.0 copy-start
  0.0 3.5 %pack.1 = bf16[3328,128]{1,0:T(8,128)(2,1)} custom-call(s32[1]{0:T(128)} %bitcast.h_ref, bf16[4096,128]{1,0:T(8,128)(2,1)} %bitcast.20, bf16[384,1536]{1,0:T(8,128)(2,1)} %bitcast.28), custom_call_target="tpu_custom_call" | custom-call | tf_op jit(solution)/shard_map/pack/pallas_call | solution.py:367
  3.5 15.2 %all-to-all-start = ((bf16[128,13,2,128]{3,2,1,0:T(2,128)(2,1)}), bf16[128,13,2,128]{3,2,1,0:T(2,128)(2,1)S(1)}, u32[]{:S(2)}, u32[]{:S(2)}) async-start(bf16[128,13,2,128]{3,2,1,0:T(2,128)(2,1)} %bitcast.27), calls=%async_computation | async-start | bytes 1703936 | tf_op jit(solution)/shard_map/all_to_all | solution.py:391
  18.7 0.0 copy-start.6
  18.7 0.0 copy-start.7
  18.7 2.8 %share.1 = bf16[16,128,768]{2,1,0:T(8,128)(2,1)} custom-call(s32[1]{0:T(128)} %bitcast.13.first_ref, bf16[32,128,768]{2,1,0:T(8,128)(2,1)} %bitcast.25), custom_call_target="tpu_custom_call" | custom-call | tf_op jit(solution)/shard_map/share/pallas_call | solution.py:376
  21.6 2.7 %collective-permute-start.2 = (bf16[16,128,768]{2,1,0:T(8,128)(2,1)}, bf16[16,128,768]{2,1,0:T(8,128)(2,1)}, u32[]{:S(2)}, u32[]{:S(2)}) collective-permute-start(bf16[16,128,768]{2,1,0:T(8,128)(2,1)} %share.1), channel_id=1, source_target_pairs={{0,17},{1,16},{2,19},{3,18},{4,21},{5,20},{6,23},{7,22},{8,25},{9,... | collective-permute-start | bytes 9437192 | tf_op jit(solution)/shard_map/ppermute | solution.py:389
  24.3 0.0 copy-done.6
  24.3 0.1 copy.13.nbr_ref
  24.4 0.5 collective-permute-start
  24.9 0.0 copy-done
  25.0 0.1 squeeze.15
  25.1 0.1 copy.12
  25.2 0.1 reshape.17.partner_ref
  25.3 0.0 copy-done.7
  25.3 3.5 %collective-permute-done = s32[32,2]{1,0:T(8,128)S(1)} collective-permute-done((s32[32,2]{1,0:T(8,128)S(1)}, s32[32,2]{1,0:T(8,128)S(1)}, u32[]{:S(2)}, u32[]{:S(2)}) %collective-permute-start) | collective-permute-done | bytes 288 | tf_op jit(solution)/shard_map/ppermute | solution.py:363
  28.9 0.7 fusion.10
  33.2 11.5 %all-to-all-done.r_ref = bf16[128,13,2,128]{3,2,1,0:T(2,128)(2,1)S(1)} async-done(((bf16[128,13,2,128]{3,2,1,0:T(2,128)(2,1)}), bf16[128,13,2,128]{3,2,1,0:T(2,128)(2,1)S(1)}, u32[]{:S(2)}, u32[]{:S(2)}) %all-to-all-start) | async-done | bytes 852000 | tf_op jit(solution)/shard_map/all_to_all | solution.py:391
  44.8 2.5 %collective-permute-start.1 = (bf16[1,9,2,128]{3,2,1,0:T(2,128)(2,1)S(1)}, bf16[1,9,2,128]{3,2,1,0:T(2,128)(2,1)S(1)}, u32[]{:S(2)}, u32[]{:S(2)}) collective-permute-start(bf16[1,9,2,128]{3,2,1,0:T(2,128)(2,1)S(1)} %get-tuple-element.29), channel_id=1, source_target_pairs={{0,1},{1,0},{2,3},{3,2},{4,5},{5,4},{6,7},{7,6},{8,9},{9,8},{10,11... | collective-permute-start | bytes 13832 | tf_op jit(solution)/shard_map/ppermute | solution.py:403
  47.3 1.6 %collective-permute-done.1.got_ref = bf16[1,9,2,128]{3,2,1,0:T(2,128)(2,1)S(1)} collective-permute-done((bf16[1,9,2,128]{3,2,1,0:T(2,128)(2,1)S(1)}, bf16[1,9,2,128]{3,2,1,0:T(2,128)(2,1)S(1)}, u32[]{:S(2)}, u32[]{:S(2)}) %collective-permute-start.1) | collective-permute-done | bytes 4640 | tf_op jit(solution)/shard_map/ppermute | solution.py:403
  48.9 1.9 %route.1 = bf16[128,13,2,128]{3,2,1,0:T(2,128)(2,1)} custom-call(s32[1]{0:T(128)} %bitcast.h_ref, s32[128]{0:T(128)S(1)} %reshape.17.partner_ref, bf16[128,13,2,128]{3,2,1,0:T(2,128)(2,1)S(1)} %all-to-all-done.r_ref, bf16[1,9,2,128]{3,2,1,0:T(2,128)(2,1)S(1)} %get-tuple-element.30.own_ref, bf16[1,9,2,128]{3,2,1,0:T(2,128)(2,1)S(1)} %collective-permute-done.1.got_ref), custom_call_target="tpu_custom_call" | custom-call | tf_op jit(solution)/shard_map/route/pallas_call | solution.py:404
  50.8 7.2 %all-to-all-start.1 = ((bf16[128,13,2,128]{3,2,1,0:T(2,128)(2,1)}), bf16[128,13,2,128]{3,2,1,0:T(2,128)(2,1)S(1)}, u32[]{:S(2)}, u32[]{:S(2)}) async-start(bf16[128,13,2,128]{3,2,1,0:T(2,128)(2,1)} %route.1), calls=%async_computation.1 | async-start | bytes 1703936 | tf_op jit(solution)/shard_map/all_to_all | solution.py:412
  58.0 26.0 %all-to-all-done.1 = bf16[128,13,2,128]{3,2,1,0:T(2,128)(2,1)S(1)} async-done(((bf16[128,13,2,128]{3,2,1,0:T(2,128)(2,1)}), bf16[128,13,2,128]{3,2,1,0:T(2,128)(2,1)S(1)}, u32[]{:S(2)}, u32[]{:S(2)}) %all-to-all-start.1) | async-done | bytes 852000 | tf_op jit(solution)/shard_map/all_to_all | solution.py:412
  84.1 1.2 %slice.8 = bf16[128,9,2,128]{3,2,1,0:T(2,128)(2,1)} slice(bf16[128,13,2,128]{3,2,1,0:T(2,128)(2,1)S(1)} %all-to-all-done.1), slice={[0:128], [4:13], [0:2], [0:128]} | slice | bytes 1179648 | tf_op jit(solution)/shard_map/slice | solution.py:414
  85.3 0.2 slice.9
  85.5 0.0 copy-start.2
  85.5 1.2 %copy-done.2 = bf16[1,4096,128]{2,1,0:T(8,128)(2,1)S(1)} copy-done((bf16[1,4096,128]{2,1,0:T(8,128)(2,1)S(1)}, bf16[1,4096,128]{2,1,0:T(8,128)(2,1)}, u32[]{:S(2)}) %copy-start.2) | copy-done | bytes 1048600
  86.7 8.0 %pair_products.3 = (bf16[16,768,128]{2,1,0:T(8,128)(2,1)S(1)}, bf16[64,32,128]{2,1,0:T(8,128)(2,1)S(1)}, f32[8,128]{1,0:T(8,128)S(1)}) custom-call(s32[1]{0:T(128)} %bitcast.4.s_ref, s32[32,2]{1,0:T(8,128)S(1)} %copy.13.nbr_ref, bf16[1024,128]{1,0:T(8,128)(2,1)S(1)} %bitcast.24, bf16[32,128,768]{2,1,0:T(8,128)(2,1)} %bitcast.26, bf16[4096,128]{1,0:T(8,128)(2,1)S(1)} %bitcast.21), custom_call_target="tpu_custom_call" | custom-call | flops 6400000000 | bytes 8000000 | tf_op jit(solution)/shard_map/pair_products/pallas_call | solution.py:214
  94.7 0.0 copy-start.4
  94.7 0.8 copy-done.4
  95.5 0.0 collective-permute-done.2.rest_0_
  95.5 0.4 collective-permute-start.3
  95.9 0.1 pad_add_fusion.s_ref
  96.0 0.3 collective-permute-start.4
  96.3 0.0 copy-start.3
  96.3 1.2 %copy-done.3 = bf16[1,4096,128]{2,1,0:T(8,128)(2,1)S(1)} copy-done((bf16[1,4096,128]{2,1,0:T(8,128)(2,1)S(1)}, bf16[1,4096,128]{2,1,0:T(8,128)(2,1)}, u32[]{:S(2)}) %copy-start.3) | copy-done | bytes 1048600
  97.5 0.0 copy-start.5
  97.5 1.0 copy-done.5
  98.6 4.8 %pair_products.4.rest_2_ = bf16[16,768,128]{2,1,0:T(8,128)(2,1)S(1)} custom-call(s32[1]{0:T(128)} %bitcast.14.s_ref, s32[16,2]{1,0:T(8,128)S(1)} %get-tuple-element.31.nbr_ref, bf16[64,32,128]{2,1,0:T(8,128)(2,1)S(1)} %copy-done.5, bf16[16,128,768]{2,1,0:T(8,128)(2,1)} %collective-permute-done.2.rest_0_, ...), custom_call_target="tpu_custom_call", output_to_operand_aliasing={{}: (5, {})} | custom-call | flops 3200000000 | bytes 4000000 | tf_op jit(solution)/shard_map/pair_products/pallas_call | solution.py:214
  103.4 0.0 collective-permute-done.3.rest_0_
  103.4 0.0 copy-start.1
  103.4 4.8 %pair_products.5.p_ref = bf16[16,768,128]{2,1,0:T(8,128)(2,1)S(1)} custom-call(s32[1]{0:T(128)} %bitcast.2.s_ref, s32[16,2]{1,0:T(8,128)S(1)} %get-tuple-element.32.nbr_ref, bf16[64,32,128]{2,1,0:T(8,128)(2,1)S(1)} %copy-done.5, bf16[16,128,768]{2,1,0:T(8,128)(2,1)} %collective-permute-done.3.rest_0_, ...), custom_call_target="tpu_custom_call", output_to_operand_aliasing={{}: (5, {})} | custom-call | flops 3200000000 | bytes 4000000 | tf_op jit(solution)/shard_map/pair_products/pallas_call | solution.py:214
  108.3 0.0 collective-permute-done.4.wb_ref
  108.3 0.0 copy-done.1
  108.3 5.8 %screened_sigma.1 = (f32[32,128]{1,0:T(8,128)S(1)}, f32[32,128]{1,0:T(8,128)S(1)}) custom-call(s32[2]{0:T(128)S(1)} %pad_add_fusion.s_ref, bf16[16,768,128]{2,1,0:T(8,128)(2,1)S(1)} %pair_products.5.p_ref, bf16[2304,128]{1,0:T(8,128)(2,1)S(1)} %bitcast.19, bf16[2304,128]{1,0:T(8,128)(2,1)S(1)} %collective-permute-done.4.wb_ref), custom_call_target="tpu_custom_call" | custom-call | tf_op jit(solution)/shard_map/screened_sigma/pallas_call | solution.py:307
  114.1 2.5 %collective-permute-start.5 = (f32[32,128]{1,0:T(8,128)S(1)}, f32[32,128]{1,0:T(8,128)S(1)}, u32[]{:S(2)}, u32[]{:S(2)}) collective-permute-start(f32[32,128]{1,0:T(8,128)S(1)} %get-tuple-element.28), channel_id=1, source_target_pairs={{0,1},{1,0},{2,3},{3,2},{4,5},{5,4},{6,7},{7,6},{8,9},{9,8},{10,11... | collective-permute-start | bytes 49160 | tf_op jit(solution)/shard_map/ppermute | solution.py:430
  116.6 1.6 %collective-permute-done.5 = f32[32,128]{1,0:T(8,128)S(1)} collective-permute-done((f32[32,128]{1,0:T(8,128)S(1)}, f32[32,128]{1,0:T(8,128)S(1)}, u32[]{:S(2)}, u32[]{:S(2)}) %collective-permute-start.5) | collective-permute-done | bytes 16416 | tf_op jit(solution)/shard_map/ppermute | solution.py:430
  118.3 0.6 add_bitcast_fusion
  (5 shorter events, 0.1 us)
Async XLA Ops:
  0.0 24.9 %copy-start = (s32[2,128]{1,0:T(2,128)S(1)}, s32[2,128]{1,0:T(2,128)}, u32[]{:S(2)}) copy-start(s32[2,128]{1,0:T(2,128)} %param.10) | copy-start | bytes 3076
  3.5 41.2 %all-to-all-start = ((bf16[128,13,2,128]{3,2,1,0:T(2,128)(2,1)}), bf16[128,13,2,128]{3,2,1,0:T(2,128)(2,1)S(1)}, u32[]{:S(2)}, u32[]{:S(2)}) async-start(bf16[128,13,2,128]{3,2,1,0:T(2,128)(2,1)} %bitcast.27), calls=%async_computation | async-start | bytes 1703936 | tf_op jit(solution)/shard_map/all_to_all | solution.py:391
  18.7 5.6 %copy-start.6 = (s32[32,2]{0,1:T(2,128)S(1)}, s32[32,2]{0,1:T(2,128)}, u32[]{:S(2)}) copy-start(s32[32,2]{0,1:T(2,128)} %param.8) | copy-start | bytes 772
  18.7 6.6 %copy-start.7 = (s32[2]{0:T(128)S(1)}, s32[2]{0:T(128)}, u32[]{:S(2)}) copy-start(s32[2]{0:T(128)} %param.11) | copy-start | bytes 28
  21.6 73.9 %collective-permute-start.2 = (bf16[16,128,768]{2,1,0:T(8,128)(2,1)}, bf16[16,128,768]{2,1,0:T(8,128)(2,1)}, u32[]{:S(2)}, u32[]{:S(2)}) collective-permute-start(bf16[16,128,768]{2,1,0:T(8,128)(2,1)} %share.1), channel_id=1, source_target_pairs={{0,17},{1,16},{2,19},{3,18},{4,21},{5,20},{6,23},{7,22},{8,25},{9,... | collective-permute-start | bytes 9437192 | tf_op jit(solution)/shard_map/ppermute | solution.py:389
  24.4 4.5 %collective-permute-start = (s32[32,2]{1,0:T(8,128)S(1)}, s32[32,2]{1,0:T(8,128)S(1)}, u32[]{:S(2)}, u32[]{:S(2)}) collective-permute-start(s32[32,2]{1,0:T(8,128)S(1)} %copy.13.nbr_ref), channel_id=1, source_target_pairs={{0,1},{1,0},{2,3},{3,2},{4,5},{5,4},{6,7},{7,6},{8,9},{9,8},{10,11... | collective-permute-start | bytes 776 | tf_op jit(solution)/shard_map/ppermute | solution.py:363
  44.8 4.2 %collective-permute-start.1 = (bf16[1,9,2,128]{3,2,1,0:T(2,128)(2,1)S(1)}, bf16[1,9,2,128]{3,2,1,0:T(2,128)(2,1)S(1)}, u32[]{:S(2)}, u32[]{:S(2)}) collective-permute-start(bf16[1,9,2,128]{3,2,1,0:T(2,128)(2,1)S(1)} %get-tuple-element.29), channel_id=1, source_target_pairs={{0,1},{1,0},{2,3},{3,2},{4,5},{5,4},{6,7},{7,6},{8,9},{9,8},{10,11... | collective-permute-start | bytes 13832 | tf_op jit(solution)/shard_map/ppermute | solution.py:403
  50.8 33.3 %all-to-all-start.1 = ((bf16[128,13,2,128]{3,2,1,0:T(2,128)(2,1)}), bf16[128,13,2,128]{3,2,1,0:T(2,128)(2,1)S(1)}, u32[]{:S(2)}, u32[]{:S(2)}) async-start(bf16[128,13,2,128]{3,2,1,0:T(2,128)(2,1)} %route.1), calls=%async_computation.1 | async-start | bytes 1703936 | tf_op jit(solution)/shard_map/all_to_all | solution.py:412
  85.5 1.2 %copy-start.2 = (bf16[1,4096,128]{2,1,0:T(8,128)(2,1)S(1)}, bf16[1,4096,128]{2,1,0:T(8,128)(2,1)}, u32[]{:S(2)}) copy-start(bf16[1,4096,128]{2,1,0:T(8,128)(2,1)} %param.6) | copy-start | bytes 3145732
  94.7 0.8 copy-start.4
  95.5 7.9 %collective-permute-start.3 = (bf16[16,128,768]{2,1,0:T(8,128)(2,1)}, bf16[16,128,768]{2,1,0:T(8,128)(2,1)}, u32[]{:S(2)}, u32[]{:S(2)}) collective-permute-start(bf16[16,128,768]{2,1,0:T(8,128)(2,1)} %collective-permute-done.2.rest_0_), channel_id=1, source_target_pairs={{0,2},{2,0},{1,3},{3,1},{4,6},{6,4},{5,7},{7,5},{8,10},{10,8},{9,1... | collective-permute-start | bytes 9437192 | tf_op jit(solution)/shard_map/ppermute | solution.py:421
  96.0 12.3 %collective-permute-start.4 = (bf16[2304,128]{1,0:T(8,128)(2,1)}, bf16[2304,128]{1,0:T(8,128)(2,1)S(1)}, u32[]{:S(2)}, u32[]{:S(2)}) collective-permute-start(bf16[2304,128]{1,0:T(8,128)(2,1)} %bitcast.18), channel_id=1, source_target_pairs={{0,2},{2,0},{1,3},{3,1},{4,6},{6,4},{5,7},{7,5},{8,10},{10,8},{9,1... | collective-permute-start | bytes 1769480 | tf_op jit(solution)/shard_map/ppermute | solution.py:417
  96.3 1.2 %copy-start.3 = (bf16[1,4096,128]{2,1,0:T(8,128)(2,1)S(1)}, bf16[1,4096,128]{2,1,0:T(8,128)(2,1)}, u32[]{:S(2)}) copy-start(bf16[1,4096,128]{2,1,0:T(8,128)(2,1)} %param.6) | copy-start | bytes 3145732
  97.5 1.0 copy-start.5
  103.4 4.9 %copy-start.1 = (bf16[128,9,2,128]{3,2,1,0:T(2,128)(2,1)S(1)}, bf16[128,9,2,128]{3,2,1,0:T(2,128)(2,1)}, u32[]{:S(2)}) copy-start(bf16[128,9,2,128]{3,2,1,0:T(2,128)(2,1)} %slice.8) | copy-start | bytes 1769476
  114.1 4.2 %collective-permute-start.5 = (f32[32,128]{1,0:T(8,128)S(1)}, f32[32,128]{1,0:T(8,128)S(1)}, u32[]{:S(2)}, u32[]{:S(2)}) collective-permute-start(f32[32,128]{1,0:T(8,128)S(1)} %get-tuple-element.28), channel_id=1, source_target_pairs={{0,1},{1,0},{2,3},{3,2},{4,5},{5,4},{6,7},{7,6},{8,9},{9,8},{10,11... | collective-permute-start | bytes 49160 | tf_op jit(solution)/shard_map/ppermute | solution.py:430
